TPU v7x, 512 devices: a whole 4x8x8 slice. The times are simulated.
512 devices in a mesh: expert: 64 (over x, z, core), dp: 8 (over y).
Axes of the slice: x: 4, y: 8, z: 8, core: 2. Of those that a mesh axis runs over, the one named last changes fastest.
Arguments:
- tokens: bfloat16 [16384, 6144], P('expert', 'dp'), may hold values from -6 to 6
- grad_out: bfloat16 [16384, 6144], P('expert', 'dp'), may hold values from -0.625 to 0.625
- combine: bfloat16 [16384, 2], P('expert'), may hold values from 0.049804688 to 1
- routes: int32 [16384, 2], P('expert'), may hold values from 0 to 63, all different within a row; in each aligned block of 256 rows (0 to 255, 256 to 511, ...) at most 9 rows name the same one
- w_gate: bfloat16 [64, 256, 6144], P('expert', None, 'dp'), may hold values from -0.078125 to 0.078125
- w_up: bfloat16 [64, 256, 6144], P('expert', None, 'dp'), may hold values from -0.078125 to 0.078125
- w_down: bfloat16 [64, 256, 6144], P('expert', None, 'dp'), may hold values from -0.375 to 0.375
Outputs:
- grad_gate: bfloat16 [64, 256, 6144], P('expert', None, 'dp')
- grad_up: bfloat16 [64, 256, 6144], P('expert', None, 'dp')
- grad_down: bfloat16 [64, 256, 6144], P('expert', None, 'dp')
- grad_combine: float32 [16384, 2], P('expert')
Inputs may be any that keep to these rules, and one draw needn't show every extreme that they name: `routes`: each token names 2 different experts. Among the tokens of one index of the expert axis no expert is named by more than 9 tokens, and on some index one expert is named by exactly 9 tokens.
All inputs are finite; a program needn't handle non-finite values.
Results may differ from a plain program's by a relative error of at most 0.0049.
Values may be sent and summed in bfloat16 or wider, within the bound.
No kernel may reach another device: no remote copies, remote signals or barrier semaphores. Data moves between devices by JAX's collectives and lax.ppermute only.
A program may use at most 64 MiB of HBM per device.

v0:
```python
import jax
import jax.numpy as jnp
from jax import lax
from jax.sharding import PartitionSpec as P

inner_dims = (((1,), (1,)), ((), ()))
outer_dims = (((0,), (0,)), ((), ()))


def silu_parts(gate_pre):
    sig_val = jax.nn.sigmoid(gate_pre)
    return (gate_pre * sig_val, sig_val * (1.0 + gate_pre * (1.0 - sig_val)))


def row_terms(gate_pre, up_pre, grad_hid, rows_p):
    silu_out, silu_slope = silu_parts(gate_pre)
    hidden = silu_out * up_pre
    weight = rows_p.astype(jnp.float32)[:, None]
    weighted = (weight * hidden).astype(jnp.bfloat16)
    scaled = weight * grad_hid
    up_rows = (scaled * silu_out).astype(jnp.bfloat16)
    gate_rows = (scaled * up_pre * silu_slope).astype(jnp.bfloat16)
    scores = jnp.sum(hidden * grad_hid, axis=1)
    return (gate_rows, up_rows, weighted, scores)


def local(tokens, grad_out, combine, routes, w_gate, w_up, w_down):
    tok_count, col_width = tokens.shape
    top_count = routes.shape[1]
    expert_count = lax.axis_size("expert")
    capacity = max(2, (9 * tok_count * top_count + 8 * expert_count - 1) // (8 * expert_count))
    assigned = tok_count * top_count
    slot_rows = expert_count * capacity
    flat_expert = routes.reshape(-1)
    onehot = (flat_expert[:, None] == jnp.arange(expert_count, dtype=jnp.int32)[None, :]).astype(
        jnp.int32
    )
    before = jnp.cumsum(onehot, axis=0) - onehot
    ranking = jnp.sum(before * onehot, axis=1)
    slot_of = flat_expert * capacity + ranking
    matches = slot_of[None, :] == jnp.arange(slot_rows, dtype=jnp.int32)[:, None]
    filled = jnp.any(matches, axis=1)
    source = jnp.sum(jnp.where(matches, jnp.arange(assigned, dtype=jnp.int32)[None, :], 0), axis=1)
    token_of = source // top_count
    zero_value = jnp.zeros((), jnp.bfloat16)
    tok_slots = jnp.where(filled[:, None], tokens[token_of], zero_value).reshape(
        expert_count, capacity, col_width
    )
    grad_slots = jnp.where(filled[:, None], grad_out[token_of], zero_value).reshape(
        expert_count, capacity, col_width
    )
    prob_slots = jnp.where(filled, combine.reshape(-1)[source], zero_value).reshape(
        expert_count, capacity
    )
    recv_x, recv_dy, recv_p = (
        lax.all_to_all(tok_slots, "expert", split_axis=0, concat_axis=0, tiled=True),
        lax.all_to_all(grad_slots, "expert", split_axis=0, concat_axis=0, tiled=True),
        lax.all_to_all(prob_slots, "expert", split_axis=0, concat_axis=0, tiled=True),
    )
    rows_x = recv_x.reshape(slot_rows, col_width)
    rows_dy = recv_dy.reshape(slot_rows, col_width)
    rows_p = recv_p.reshape(slot_rows)
    gate_w, up_w, down_w = (w_gate[0], w_up[0], w_down[0])
    gate_pre = lax.dot_general(rows_x, gate_w, inner_dims, preferred_element_type=jnp.float32)
    up_pre = lax.dot_general(rows_x, up_w, inner_dims, preferred_element_type=jnp.float32)
    grad_hid = lax.dot_general(rows_dy, down_w, inner_dims, preferred_element_type=jnp.float32)
    gate_sum, up_sum, grad_sum = lax.psum((gate_pre, up_pre, grad_hid), "dp")
    gate_rows, up_rows, weighted, scores = row_terms(gate_sum, up_sum, grad_sum, rows_p)
    outputs = (
        lax.dot_general(gate_rows, rows_x, outer_dims, preferred_element_type=jnp.float32),
        lax.dot_general(up_rows, rows_x, outer_dims, preferred_element_type=jnp.float32),
        lax.dot_general(weighted, rows_dy, outer_dims, preferred_element_type=jnp.float32),
    )
    returned = lax.all_to_all(
        scores.reshape(expert_count, capacity), "expert", split_axis=0, concat_axis=0, tiled=True
    )
    grad_combine = returned.reshape(-1)[slot_of].reshape(tok_count, top_count)
    return tuple((matrix.astype(jnp.bfloat16)[None] for matrix in outputs)) + (grad_combine,)


def solution(mesh):
    placed = (
        P("expert", "dp"),
        P("expert", "dp"),
        P("expert", None),
        P("expert", None),
        P("expert", None, "dp"),
        P("expert", None, "dp"),
        P("expert", None, "dp"),
    )
    return jax.shard_map(
        local,
        mesh=mesh,
        in_specs=placed,
        out_specs=(
            P("expert", None, "dp"),
            P("expert", None, "dp"),
            P("expert", None, "dp"),
            P("expert", None),
        ),
        check_vma=False,
    )
```

profile of v0, /device:TPU:1, one launch (start us, length us, event | category | flops | bytes accessed | tf_op | source)
XLA Modules:
  0.0 247.4 jit_solution(4236457712508041742)
XLA Ops:
  7.2 0.0 copy-start
  7.2 0.9 copy.25
  8.0 0.1 eq.39
  8.2 0.1 reshape.199
  8.4 1.2 reduce-window.6
  9.6 0.2 slice_reduce_fusion
  9.8 0.1 fusion.18
  10.0 0.2 select_reduce_fusion
  10.2 0.2 fusion.3
  10.5 0.0 copy-done
  10.5 3.3 %gather_fusion.1 = bf16[576,768]{1,0:T(8,128)(2,1)} fusion(bf16[256,768]{1,0:T(8,128)(2,1)S(1)} %copy-done, s32[1024]{0:T(1024)S(1)} %get-tuple-element.23), kind=kCustom, calls=%fused_computation.1 | custom fusion | bytes 1771776 | tf_op jit(solution)/shard_map/gather | solution.py:49
  13.8 1.4 gather.18
  15.2 0.0 copy-done.1
  15.3 3.3 %gather_fusion.2 = bf16[576,768]{1,0:T(8,128)(2,1)} fusion(bf16[256,768]{1,0:T(8,128)(2,1)S(1)} %copy-done.1, s32[1024]{0:T(1024)S(1)} %get-tuple-element.23), kind=kCustom, calls=%fused_computation.2 | custom fusion | bytes 1771776 | tf_op jit(solution)/shard_map/gather | solution.py:46
  18.6 2.3 gather.20
  20.9 0.1 broadcast_in_dim.57
  21.1 2.9 %broadcast_select_fusion.1 = (bf16[64,9,768]{2,1,0:T(8,128)(2,1)}, bf16[64,9,768]{2,1,0:T(8,128)(2,1)S(1)}) fusion(bf16[64,9,768]{2,1,0:T(8,128)(2,1)S(1)} %gather.18, pred[64,9]{1,0:T(8,128)(4,1)S(1)} %broadcast_in_dim.57, bf16[64,9,768]{2,1,0:T(8,128)(2,1)} %gather.20), kind=kLoop, calls=%fused_computation.5 | loop fusion | flops 884736 | bytes 3539520 | tf_op jit(solution)/shard_map/jit(_where)/select_n | solution.py:49
  23.9 54.5 %all_to_all.25 = bf16[64,9,768]{2,1,0:T(8,128)(2,1)} all-to-all(bf16[64,9,768]{2,1,0:T(8,128)(2,1)S(1)} %get-tuple-element.22), channel_id=1, replica_groups=mesh['expert'=64,'dp'=8] {'expert'}, dimensions={0} | all-to-all | bytes 1769472 | tf_op jit(solution)/shard_map/all_to_all | solution.py:56
  78.5 6.1 %all-to-all-start.1 = ((bf16[64,9,768]{2,1,0:T(8,128)(2,1)}), bf16[64,9,768]{2,1,0:T(8,128)(2,1)S(1)}, u32[]{:S(2)}, u32[]{:S(2)}) async-start(bf16[64,9,768]{2,1,0:T(8,128)(2,1)} %get-tuple-element.21), calls=%async_computation.1 | async-start | bytes 3145728 | tf_op jit(solution)/shard_map/all_to_all | solution.py:57
  84.6 0.0 copy-start.6
  84.6 0.0 all-reduce.3.cloned.1.call-start
  84.7 1.6 reshape.203
  86.3 0.0 copy-done.6
  86.3 0.0 copy-start.7
  86.3 1.2 fusion.5
  87.5 0.0 copy-done.7
  87.6 1.2 fusion.7
  88.8 35.6 %all-to-all-done.1 = bf16[64,9,768]{2,1,0:T(8,128)(2,1)S(1)} async-done(((bf16[64,9,768]{2,1,0:T(8,128)(2,1)}), bf16[64,9,768]{2,1,0:T(8,128)(2,1)S(1)}, u32[]{:S(2)}, u32[]{:S(2)}) %all-to-all-start.1) | async-done | bytes 884768 | tf_op jit(solution)/shard_map/all_to_all | solution.py:57
  124.4 1.2 reshape.202
  125.6 0.0 copy-done.8
  125.6 2.4 fusion.9
  128.0 0.0 all-reduce.3.cloned.1.call-update
  128.0 0.0 copy-done.10
  128.0 0.0 copy-start.9
  128.0 0.1 copy.28
  128.2 0.2 reshape.201
  128.3 3.9 %gather_fusion = bf16[576]{0:T(1024)(128)(2,1)S(1)} fusion(bf16[512]{0:T(512)(128)(2,1)S(1)} %reshape.201, s32[1024]{0:T(1024)S(1)} %get-tuple-element.24), kind=kCustom, calls=%fused_computation | custom fusion | bytes 4608 | tf_op jit(solution)/shard_map/gather | solution.py:52
  132.3 0.0 copy-start.2
  132.3 0.8 select_n.80
  133.1 6.1 %all-to-all-start = ((bf16[64,1,9]{2,1,0:T(2,128)(2,1)}), bf16[64,1,9]{2,1,0:T(2,128)(2,1)S(1)}, u32[]{:S(2)}, u32[]{:S(2)}) async-start(bf16[64,1,9]{2,1,0:T(2,128)(2,1)} %select_n.80), calls=%async_computation | async-start | bytes 65536 | tf_op jit(solution)/shard_map/all_to_all | solution.py:58
  139.2 0.0 copy-done.9
  139.2 0.1 copy.31
  139.4 0.1 mul.81
  139.6 8.9 %all-to-all-done = bf16[64,1,9]{2,1,0:T(2,128)(2,1)S(1)} async-done(((bf16[64,1,9]{2,1,0:T(2,128)(2,1)}), bf16[64,1,9]{2,1,0:T(2,128)(2,1)S(1)}, u32[]{:S(2)}, u32[]{:S(2)}) %all-to-all-start) | async-done | bytes 1184 | tf_op jit(solution)/shard_map/all_to_all | solution.py:58
  148.4 0.1 convert_reduce_fusion
  148.5 0.1 reshape.206
  148.7 57.9 %all-reduce.3.cloned.1.call-done = (f32[576,256]{1,0:T(8,128)}, f32[576,256]{1,0:T(8,128)}, f32[576,256]{1,0:T(8,128)}) async-done(((f32[576,256]{1,0:T(8,128)}, f32[576,256]{1,0:T(8,128)}, f32[576,256]{1,0:T(8,128)}), (f32[576,256]{1,0:T(8,128)}, f32[576,256]{1,0:T(8,128)}, f32[576,256]{1,0:T(8,128)})) %all-reduce.3.cloned.1.call-update) | async-done | bytes 1769488 | tf_op jit(solution)/shard_map/psum | solution.py:67
  206.5 1.8 multiply_reduce_fusion
  208.3 0.0 copy-done.2
  208.3 0.0 copy-done.3
  208.3 0.0 copy-done.5
  208.3 0.0 copy-start.4
  208.4 1.4 fusion.2
  209.8 1.4 fusion
  211.2 0.7 all_to_all.19
  211.9 14.9 %all-to-all-start.3 = ((f32[64,1,9]{2,1,0:T(1,128)}), f32[64,1,9]{2,1,0:T(1,128)S(1)}, u32[]{:S(2)}, u32[]{:S(2)}) async-start(f32[64,1,9]{2,1,0:T(1,128)} %bitcast.7), calls=%async_computation.3 | async-start | bytes 65536 | tf_op jit(solution)/shard_map/all_to_all | solution.py:74
  226.8 1.4 fusion.1
  228.2 7.9 %all-to-all-done.3 = f32[64,1,9]{2,1,0:T(1,128)S(1)} async-done(((f32[64,1,9]{2,1,0:T(1,128)}), f32[64,1,9]{2,1,0:T(1,128)S(1)}, u32[]{:S(2)}, u32[]{:S(2)}) %all-to-all-start.3) | async-done | bytes 2336 | tf_op jit(solution)/shard_map/all_to_all | solution.py:74
  236.1 0.5 broadcast.185
  236.6 0.7 reduce.13
  237.4 0.1 reshape.204
  237.5 2.3 gather_fusion.3
  239.8 0.1 reshape.205
  239.9 0.7 copy.32
  (16 shorter events, 0.1 us)
Async XLA Ops:
  7.2 3.3 %copy-start = (bf16[256,768]{1,0:T(8,128)(2,1)S(1)}, bf16[256,768]{1,0:T(8,128)(2,1)}, u32[]{:S(2)}) copy-start(bf16[256,768]{1,0:T(8,128)(2,1)} %param.8) | copy-start | bytes 1179652
  13.8 1.5 copy-start.1
  78.5 45.9 %all-to-all-start.1 = ((bf16[64,9,768]{2,1,0:T(8,128)(2,1)}), bf16[64,9,768]{2,1,0:T(8,128)(2,1)S(1)}, u32[]{:S(2)}, u32[]{:S(2)}) async-start(bf16[64,9,768]{2,1,0:T(8,128)(2,1)} %get-tuple-element.21), calls=%async_computation.1 | async-start | bytes 3145728 | tf_op jit(solution)/shard_map/all_to_all | solution.py:57
  84.6 1.7 copy-start.6
  84.6 121.9 %all-reduce.3.cloned.1.call-start = ((), (), s32[]{:S(2)}) async-start(), calls=%async_computation.4 | async-start | bytes 3538944 | tf_op jit(solution)/shard_map/psum | solution.py:67
  86.3 1.3 copy-start.7
  88.8 36.8 %copy-start.8 = (bf16[1,256,768]{2,1,0:T(8,128)(2,1)S(1)}, bf16[1,256,768]{2,1,0:T(8,128)(2,1)}, u32[]{:S(2)}) copy-start(bf16[1,256,768]{2,1,0:T(8,128)(2,1)} %param.13) | copy-start | bytes 1179652
  125.6 2.4 copy-start.10
  128.0 11.2 %copy-start.9 = (s32[256,2]{0,1:T(2,128)S(1)}, s32[256,2]{0,1:T(2,128)}, u32[]{:S(2)}) copy-start(s32[256,2]{0,1:T(2,128)} %param.10) | copy-start | bytes 6148
  132.3 76.0 %copy-start.2 = (bf16[576,768]{1,0:T(8,128)(2,1)S(1)}, bf16[576,768]{1,0:T(8,128)(2,1)}, u32[]{:S(2)}) copy-start(bf16[576,768]{1,0:T(8,128)(2,1)} %reshape.202) | copy-start | bytes 2654212
  133.1 15.3 %all-to-all-start = ((bf16[64,1,9]{2,1,0:T(2,128)(2,1)}), bf16[64,1,9]{2,1,0:T(2,128)(2,1)S(1)}, u32[]{:S(2)}, u32[]{:S(2)}) async-start(bf16[64,1,9]{2,1,0:T(2,128)(2,1)} %select_n.80), calls=%async_computation | async-start | bytes 65536 | tf_op jit(solution)/shard_map/all_to_all | solution.py:58
  206.5 1.8 copy-start.3
  206.5 1.8 copy-start.5
  208.3 1.4 copy-start.4
  211.9 24.2 %all-to-all-start.3 = ((f32[64,1,9]{2,1,0:T(1,128)}), f32[64,1,9]{2,1,0:T(1,128)S(1)}, u32[]{:S(2)}, u32[]{:S(2)}) async-start(f32[64,1,9]{2,1,0:T(1,128)} %bitcast.7), calls=%async_computation.3 | async-start | bytes 65536 | tf_op jit(solution)/shard_map/all_to_all | solution.py:74
Sparse Core Ops, SparseCore 0:
  128.1 78.3 all-reduce.2
where the time goes:
time: 248 us; the launch traced here: 247 us
  waiting for transfers between devices  110 us (44%)
  blocking collectives  54.5 us (22%)
  starting transfers between devices  27.2 us (11%)
  local copies, waits for them, and re-layouts  24.7 us (10%)
  between operations  14.3 us (6%)
  matrix products  9.13 us (4%)
  other arithmetic  7.34 us (3%)
    psum x1, waiting for transfers between devices, local(): gate_sum, up_sum, grad_sum = lax.psum((gate_pre, up_pre, grad_hid), 'dp')  57.9 us
    all_to_all x1, blocking collectives, local(): lax.all_to_all(tok_slots, 'expert', split_axis=0, concat_axis=0, tiled=True)  54.5 us
    all_to_all x1, waiting for transfers between devices, local(): lax.all_to_all(grad_slots, 'expert', split_axis=0, concat_axis=0, tiled=T...  35.6 us
    all_to_all x1, starting transfers between devices, local(): lax.all_to_all(scores.reshape(expert_count, capacity), 'expert', split_ax...  14.9 us
    all_to_all x1, waiting for transfers between devices, local(): lax.all_to_all(prob_slots, 'expert', split_axis=0, concat_axis=0, tiled=T...  8.87 us
    all_to_all x1, waiting for transfers between devices, local(): lax.all_to_all(scores.reshape(expert_count, capacity), 'expert', split_ax...  7.89 us
    all_to_all x1, starting transfers between devices, local(): lax.all_to_all(prob_slots, 'expert', split_axis=0, concat_axis=0, tiled=T...  6.12 us
    all_to_all x1, starting transfers between devices, local(): lax.all_to_all(grad_slots, 'expert', split_axis=0, concat_axis=0, tiled=T...  6.12 us
  transfers between devices with their start and end apart: 4, of which 4 were waited for; matrix products, arithmetic and copies ran while one was open for 4% of the time, Pallas kernels for 0%

commit v1 on v0

v1 whole, which is shorter than its diff:
```python
import functools

import jax
import jax.numpy as jnp
from jax import lax
from jax.experimental import pallas as pl
from jax.experimental.pallas import tpu as pltpu
from jax.sharding import PartitionSpec as P

bf16, f32, i32 = jnp.bfloat16, jnp.float32, jnp.int32
LANES, SUB = 128, 8
CAP = 9
LIMIT = 32 * 2**20


def params():
    return pltpu.CompilerParams(vmem_limit_bytes=LIMIT)


def iota(shape, dim):
    return lax.broadcasted_iota(i32, shape, dim)


def mm(a, b, contract=((1,), (0,))):
    return lax.dot_general(a, b, (contract, ((), ())), preferred_element_type=f32)


def pack_kernel(routes, combine, tokens, grads, out, ranks):
    experts, toks = ranks.shape
    blocks = tokens.shape[1] // LANES
    e = iota((experts, toks), 0)
    first, second = e == routes[0:1, :], e == routes[1:2, :]
    named = first | second
    hot = jnp.where(named, 1.0, 0.0).astype(bf16)
    before = jnp.where(iota((toks, toks), 0) < iota((toks, toks), 1), 1.0, 0.0).astype(bf16)
    rank = jnp.where(named, mm(hot, before), -1.0)
    ranks[...] = rank
    prob = combine[...].astype(f32)
    prob = jnp.where(first, prob[0:1, :], jnp.where(second, prob[1:2, :], 0.0))

    slot = iota((experts, SUB, toks), 1)
    spread = jnp.broadcast_to(rank[:, None, :], (experts, SUB, toks))
    pick = jnp.where(spread == slot.astype(f32), 1.0, 0.0)
    pick = pick.reshape(experts * SUB, toks).astype(bf16)
    for i, source in enumerate((tokens, grads)):
        rows = mm(pick, source[...])
        for c in range(blocks):
            tile = rows[:, c * LANES : (c + 1) * LANES].reshape(experts, SUB, LANES)
            at = (i * blocks + c) * SUB
            out[:, at : at + SUB, :] = tile.astype(bf16)

    ninth = jnp.where(rank == float(SUB), 1.0, 0.0)
    ninth = jnp.broadcast_to(ninth[:, None, :], (experts, SUB, toks))
    places = [(tokens, c) for c in range(blocks)] + [(grads, c) for c in range(blocks)]
    at = 2 * blocks * SUB
    for base in range(0, len(places) + 1, SUB):
        total = jnp.zeros((experts * SUB, LANES), f32)
        for k, (source, c) in enumerate(places[base : base + SUB]):
            mask = jnp.where(slot == k, ninth, 0.0).reshape(experts * SUB, toks).astype(bf16)
            total = total + mm(mask, source[:, c * LANES : (c + 1) * LANES])
        total = total.reshape(experts, SUB, LANES)
        if base + SUB > len(places):
            lane = iota((experts, LANES), 1)
            row = jnp.zeros((experts, LANES), f32)
            for r in range(CAP):
                value = jnp.sum(jnp.where(rank == float(r), prob, 0.0), axis=1, keepdims=True)
                row = jnp.where(lane == r, value, row)
            row = jnp.broadcast_to(row[:, None, :], (experts, SUB, LANES))
            total = jnp.where(iota((experts, SUB, LANES), 1) == len(places) - base, row, total)
        out[:, at + base : at + base + SUB, :] = total.astype(bf16)


def pack(routes, combine, tokens, grads, experts):
    toks, width = tokens.shape
    rows = (2 * width // LANES) * SUB + 2 * SUB
    return pl.pallas_call(
        pack_kernel,
        out_shape=(
            jax.ShapeDtypeStruct((experts, rows, LANES), bf16),
            jax.ShapeDtypeStruct((experts, toks), f32),
        ),
        compiler_params=params(),
        name="pack",
    )(routes, combine, tokens, grads)


def project_kernel(me, recv, w_gate, w_up, w_down, part, own, rows_x, rows_dy, probs):
    experts = recv.shape[0]
    groups, count, _ = part.shape
    width = rows_x.shape[1]
    blocks = width // LANES
    main = experts * SUB
    share = main // groups

    def tile(at):
        return recv[:, at : at + SUB, :].astype(f32).reshape(main, LANES).astype(bf16)

    at = 2 * blocks * SUB
    last = [tile(at), tile(at + SUB)]
    column, line = iota((experts, main), 1), iota((experts, main), 0)

    def taken(index):
        pick = jnp.where(column == line * SUB + index % SUB, 1.0, 0.0).astype(bf16)
        return mm(pick, last[index // SUB])

    for i, rows in enumerate((rows_x, rows_dy)):
        for c in range(blocks):
            lanes = slice(c * LANES, (c + 1) * LANES)
            rows[0:main, lanes] = tile((i * blocks + c) * SUB)
            rows[main:, lanes] = taken(i * blocks + c).astype(bf16)
    probs[...] = taken(2 * blocks)

    x, dy = rows_x[...], rows_dy[...]
    hidden = w_gate.shape[1]
    for i, (rows, weight) in enumerate(((x, w_gate), (x, w_up), (dy, w_down))):
        lanes = slice(i * hidden, (i + 1) * hidden)
        value = mm(rows, weight[0], ((1,), (1,)))
        for j in range(groups):
            piece = jnp.concatenate(
                [value[j * share : (j + 1) * share], value[main + j * SUB : main + (j + 1) * SUB]]
            )
            part[j, :, lanes] = piece.astype(bf16)

            @pl.when(me[0] == j)
            def _(piece=piece, lanes=lanes):
                own[:, lanes] = piece


def project(me, recv, w_gate, w_up, w_down, groups):
    experts = recv.shape[0]
    hidden, width = w_gate.shape[1:]
    total = experts * CAP
    count = total // groups
    vmem = pl.BlockSpec(memory_space=pltpu.VMEM)
    return pl.pallas_call(
        project_kernel,
        in_specs=[pl.BlockSpec(memory_space=pltpu.SMEM)] + [vmem] * 4,
        out_shape=(
            jax.ShapeDtypeStruct((groups, count, 3 * hidden), bf16),
            jax.ShapeDtypeStruct((count, 3 * hidden), f32),
            jax.ShapeDtypeStruct((total, width), bf16),
            jax.ShapeDtypeStruct((total, width), bf16),
            jax.ShapeDtypeStruct((experts, LANES), f32),
        ),
        compiler_params=params(),
        name="project",
    )(me, recv, w_gate, w_up, w_down)


def terms_kernel(me, parts, own, probs, out):
    groups, count, _ = parts.shape
    hidden = parts.shape[2] // 3
    main = count - SUB
    near = probs[pl.ds(pl.multiple_of(me[0] * SUB, SUB), SUB), :]
    lane = iota((SUB, SUB, LANES), 2)
    spread = jnp.broadcast_to(near[:, None, :], (SUB, SUB, LANES))
    picked = jnp.sum(jnp.where(lane == iota((SUB, SUB, LANES), 1), spread, 0.0), axis=2, keepdims=True)
    ninth = jnp.sum(jnp.where(iota((SUB, LANES), 1) == SUB, near, 0.0), axis=1, keepdims=True)
    weight = jnp.concatenate([picked.reshape(main, 1), ninth])

    def total(i):
        lanes = slice(i * hidden, (i + 1) * hidden)
        value = own[:, lanes]
        for j in range(groups):
            value = value + jnp.where(me[0] == j, 0.0, parts[j, :, lanes].astype(f32))
        return value

    gate_pre, up_pre, grad_hid = total(0), total(1), total(2)
    sig = jax.nn.sigmoid(gate_pre)
    silu_out = gate_pre * sig
    inner = silu_out * up_pre
    scaled = weight * grad_hid
    out[:, 0:hidden] = (scaled * up_pre * (sig * (1.0 + gate_pre * (1.0 - sig)))).astype(bf16)
    out[:, hidden : 2 * hidden] = (scaled * silu_out).astype(bf16)
    out[:, 2 * hidden : 3 * hidden] = (weight * inner).astype(bf16)
    score = jnp.sum(inner * grad_hid, axis=1, keepdims=True)
    high = score.astype(bf16).astype(f32)
    middle = (score - high).astype(bf16).astype(f32)
    low = score - high - middle
    lane = iota((count, LANES), 1)
    triple = jnp.where(lane == 0, high, jnp.where(lane == 1, middle, jnp.where(lane == 2, low, 0.0)))
    out[:, 3 * hidden :] = triple.astype(bf16)


def terms(me, parts, own, probs):
    count, wide = own.shape
    vmem = pl.BlockSpec(memory_space=pltpu.VMEM)
    return pl.pallas_call(
        terms_kernel,
        in_specs=[pl.BlockSpec(memory_space=pltpu.SMEM)] + [vmem] * 3,
        out_shape=jax.ShapeDtypeStruct((count, wide + LANES), bf16),
        compiler_params=params(),
        name="terms",
    )(me, parts, own, probs)


def scores_kernel(triples, out):
    groups, count, _ = triples.shape
    main = count - SUB
    score = jnp.sum(triples[...].astype(f32), axis=2, keepdims=True)
    sources = groups * SUB
    lane, slot = iota((sources, SUB, LANES), 2), iota((sources, SUB, LANES), 1)
    direct = jnp.broadcast_to(score[:, :main].reshape(sources, SUB, 1), (sources, SUB, LANES))
    ninth = jnp.broadcast_to(score[:, main:], (groups, SUB, LANES))
    ninth = jnp.broadcast_to(ninth[:, None], (groups, SUB, SUB, LANES)).reshape(sources, SUB, LANES)
    mine = lax.rem(iota((sources, SUB, LANES), 0), SUB) == slot
    both = jnp.where(lane == slot, direct, jnp.where((lane == SUB) & mine, ninth, 0.0))
    out[...] = jnp.sum(both, axis=1, keepdims=True)


def scores_by_source(triples, sources):
    return pl.pallas_call(
        scores_kernel,
        out_shape=jax.ShapeDtypeStruct((sources, 1, LANES), f32),
        compiler_params=params(),
        name="scores",
    )(triples)


def outer_kernel(rows, rows_x, rows_dy, gate, up, down):
    groups, count, _ = rows.shape
    hidden = gate.shape[1]
    main = count - SUB
    x, dy = rows_x[...], rows_dy[...]
    for i, (other, out) in enumerate(((x, gate), (x, up), (dy, down))):
        lanes = slice(i * hidden, (i + 1) * hidden)
        direct = rows[:, 0:main, lanes].astype(f32).reshape(groups * main, hidden)
        ninth = rows[:, main:, lanes].astype(f32).reshape(groups * SUB, hidden)
        value = jnp.concatenate([direct, ninth]).astype(bf16)
        out[0] = mm(value, other, ((0,), (0,))).astype(bf16)


def outer(rows, rows_x, rows_dy, hidden):
    total, width = rows_x.shape
    return pl.pallas_call(
        outer_kernel,
        out_shape=(jax.ShapeDtypeStruct((1, hidden, width), bf16),) * 3,
        compiler_params=params(),
        cost_estimate=pl.CostEstimate(
            flops=6 * total * width * hidden, bytes_accessed=8 * total * width, transcendentals=0
        ),
        name="outer",
    )(rows, rows_x, rows_dy)


def place_kernel(routes, ranks, scores, out):
    experts, toks = ranks.shape
    spread = jnp.broadcast_to(scores[...], (experts, SUB, LANES))
    spread = spread.reshape(experts // SUB, SUB, SUB, LANES)
    mine = iota(spread.shape, 1) == iota(spread.shape, 2)
    table = jnp.sum(jnp.where(mine, spread, 0.0), axis=1).reshape(experts, LANES)
    rank = ranks[...]
    value = jnp.zeros((experts, toks), f32)
    for r in range(CAP):
        value = jnp.where(rank == float(r), table[:, r : r + 1], value)
    e = iota((experts, toks), 0)
    for k in range(2):
        out[k : k + 1, :] = jnp.sum(
            jnp.where(e == routes[k : k + 1, :], value, 0.0), axis=0, keepdims=True
        )


def place(routes, ranks, scores):
    return pl.pallas_call(
        place_kernel,
        out_shape=jax.ShapeDtypeStruct(routes.shape, f32),
        compiler_params=params(),
        name="place",
    )(routes, ranks, scores)


def local(tokens, grad_out, combine, routes, w_gate, w_up, w_down):
    experts, groups = lax.axis_size("expert"), lax.axis_size("dp")
    hidden = w_gate.shape[1]
    me = lax.axis_index("dp").astype(i32).reshape(1)
    by_slot = routes.T
    packed, ranks = pack(by_slot, combine.T, tokens, grad_out, experts)
    recv = lax.all_to_all(packed, "expert", split_axis=0, concat_axis=0, tiled=True)
    part, own, rows_x, rows_dy, probs = project(me, recv, w_gate, w_up, w_down, groups)
    parts = lax.all_to_all(part, "dp", split_axis=0, concat_axis=0, tiled=True)
    mine = terms(me, parts, own, probs)
    rows = lax.all_gather(mine, "dp", axis=0, tiled=False)
    triples = rows[:, :, 3 * hidden :]
    returned = lax.all_to_all(
        scores_by_source(triples, experts), "expert", split_axis=0, concat_axis=0, tiled=True
    )
    grads = outer(rows, rows_x, rows_dy, hidden)
    return tuple(grads) + (place(by_slot, ranks, returned).T,)


def solution(mesh):
    placed = (
        P("expert", "dp"),
        P("expert", "dp"),
        P("expert", None),
        P("expert", None),
        P("expert", None, "dp"),
        P("expert", None, "dp"),
        P("expert", None, "dp"),
    )
    return jax.shard_map(
        local,
        mesh=mesh,
        in_specs=placed,
        out_specs=(
            P("expert", None, "dp"),
            P("expert", None, "dp"),
            P("expert", None, "dp"),
            P("expert", None),
        ),
        check_vma=False,
    )
```

time: 248 us -> 149 us (0.60)
  waiting for transfers between devices: 110 us -> 51.7 us
  local copies, waits for them, and re-layouts: 24.7 us -> 8.3 us
  between operations: 14.3 us -> 0.72 us
  matrix products: 9.13 us -> 0 us
  Pallas kernels: 0 us -> 7.6 us
  other arithmetic: 7.34 us -> 0 us
    psum x1 -> x0, waiting for transfers between devices: 57.9 us -> none  [local(): gate_sum, up_sum, grad_sum = lax.psum((gate_pre, up_pre, grad_hid), 'dp')]
    all_to_all x1, blocking collectives: 54.5 us -> 31 us  [local(): parts = lax.all_to_all(part, 'dp', split_axis=0, concat_axis=0, tiled=True)]
    all_gather x0 -> x1, blocking collectives: none -> 21.4 us  [local(): rows = lax.all_gather(mine, 'dp', axis=0, tiled=False)]
    gather x6 -> x0, local copies, waits for them, and re-layouts: 16.7 us -> none  [the longest x2 5.67 us: local(): tokens[token_of]]
    dot_general x6 -> x0, matrix products: 9.13 us -> none  [the longest x1 2.42 us: local(): lax.dot_general(rows_dy, down_w, inner_dims, preferred_element_type=jnp.f...]
    pallas_call x0 -> x6, Pallas kernels: none -> 7.6 us  [the longest x1 2.32 us: project(): pl.pallas_call(project_kernel, in_specs=[pl.BlockSpec(memory_space=pltpu....]
    unnamed x25 -> x26, local copies, waits for them, and re-layouts: 1.72 us -> 8.28 us
    reshape x6 -> x0, local copies, waits for them, and re-layouts: 3.35 us -> none  [the longest x1 1.62 us: local(): rows_x = recv_x.reshape(slot_rows, col_width)]
  transfers between devices with their start and end apart: 4 -> 2, of which waited for: 4 -> 2; matrix products, arithmetic and copies ran while one was open for 4% -> 0% of each run, Pallas kernels for 0% -> 1%
where the time goes in v1:
time: 149 us; the launch traced here: 148 us
  blocking collectives  52.3 us (35%)
  waiting for transfers between devices  51.7 us (35%)
  starting transfers between devices  27.8 us (19%)
  local copies, waits for them, and re-layouts  8.3 us (6%)
  Pallas kernels  7.6 us (5%)
    all_to_all x1, waiting for transfers between devices, local(): lax.all_to_all(packed, 'expert', split_axis=0, concat_axis=0, tiled=True)  45.4 us
    all_to_all x1, blocking collectives, local(): parts = lax.all_to_all(part, 'dp', split_axis=0, concat_axis=0, tiled=True)  31 us
    all_gather x1, blocking collectives, local(): rows = lax.all_gather(mine, 'dp', axis=0, tiled=False)  21.4 us
    all_to_all x1, starting transfers between devices, local(): lax.all_to_all(packed, 'expert', split_axis=0, concat_axis=0, tiled=True)  15 us
    all_to_all x1, starting transfers between devices, local(): lax.all_to_all(scores_by_source(triples, experts), 'expert', split_axis=0...  12.9 us
    unnamed x26, local copies, waits for them, and re-layouts  8.28 us
    all_to_all x1, waiting for transfers between devices, local(): lax.all_to_all(scores_by_source(triples, experts), 'expert', split_axis=0...  6.24 us
  transfers between devices with their start and end apart: 2, of which 2 were waited for; matrix products, arithmetic and copies ran while one was open for 0% of the time, Pallas kernels for 1%

profile of v1, /device:TPU:1, one launch (start us, length us, event | category | flops | bytes accessed | tf_op | source)
XLA Modules:
  0.0 148.4 jit_solution(6621718689558273680)
XLA Ops:
  0.6 0.0 copy-start.6
  0.6 1.0 copy-done.6
  1.6 0.0 copy-start.7
  1.6 1.0 copy-done.7
  2.6 0.0 copy-start.10
  2.6 0.7 copy-done.10
  3.3 0.0 copy-start.12
  3.3 0.7 copy-done.12
  4.0 1.6 %pack.1 = (bf16[64,112,128]{2,1,0:T(8,128)(2,1)S(1)}, f32[64,256]{1,0:T(8,128)S(1)}) custom-call(s32[2,256]{1,0:T(2,128)S(1)} %bitcast.7, bf16[2,256]{1,0:T(2,128)(2,1)S(1)} %bitcast.9, bf16[256,768]{1,0:T(8,128)(2,1)S(1)} %copy-done.6, bf16[256,768]{1,0:T(8,128)(2,1)S(1)} %copy-done.7), custom_call_target="tpu_custom_call" | custom-call | tf_op jit(solution)/shard_map/pack/pallas_call | solution.py:76
  5.6 0.0 copy-start
  5.6 1.2 copy-done
  6.8 0.0 copy-start.8
  6.8 0.6 copy-done.8
  7.4 0.0 copy-start.3
  7.4 0.0 copy-start.4
  7.4 15.0 %all-to-all-start = ((bf16[64,112,128]{2,1,0:T(8,128)(2,1)}), bf16[64,112,128]{2,1,0:T(8,128)(2,1)S(1)}, u32[]{:S(2)}, u32[]{:S(2)}) async-start(bf16[64,112,128]{2,1,0:T(8,128)(2,1)} %copy-done), calls=%async_computation | async-start | bytes 3670016 | tf_op jit(solution)/shard_map/all_to_all | solution.py:278
  22.4 45.4 %all-to-all-done.recv = bf16[64,112,128]{2,1,0:T(8,128)(2,1)S(1)} async-done(((bf16[64,112,128]{2,1,0:T(8,128)(2,1)}), bf16[64,112,128]{2,1,0:T(8,128)(2,1)S(1)}, u32[]{:S(2)}, u32[]{:S(2)}) %all-to-all-start) | async-done | bytes 1835040 | tf_op jit(solution)/shard_map/all_to_all | solution.py:278
  67.8 0.0 copy-done.3
  67.8 0.0 copy-done.4
  67.8 0.0 copy-start.5
  67.8 1.0 copy-done.5
  68.8 2.3 %project.1 = (bf16[8,72,768]{2,1,0:T(8,128)(2,1)S(1)}, f32[72,768]{1,0:T(8,128)S(1)}, bf16[576,768]{1,0:T(8,128)(2,1)S(1)}, bf16[576,768]{1,0:T(8,128)(2,1)S(1)}, f32[64,128]{1,0:T(8,128)S(1)}) custom-call(s32[1]{0:T(128)} %bitcast.me, bf16[64,112,128]{2,1,0:T(8,128)(2,1)S(1)} %all-to-all-done.recv, bf16[1,256,768]{2,1,0:T(8,128)(2,1)S(1)} %copy-done.3, ...), custom_call_target="tpu_custom_call" | custom-call | tf_op jit(solution)/shard_map/project/pallas_call | solution.py:135
  71.1 0.0 copy-start.1
  71.2 0.9 copy-done.1
  72.1 31.0 %all_to_all.15.parts = bf16[8,72,768]{2,1,0:T(8,128)(2,1)S(1)} all-to-all(bf16[8,72,768]{2,1,0:T(8,128)(2,1)S(1)} %get-tuple-element.15), channel_id=1, replica_groups=mesh['expert'=64,'dp'=8] {'dp'}, dimensions={0} | all-to-all | bytes 1769472 | tf_op jit(solution)/shard_map/all_to_all | solution.py:280
  103.0 0.3 terms.1
  103.3 21.4 %all-gather = bf16[576,896]{1,0:T(8,128)(2,1)S(1)} all-gather(bf16[72,896]{1,0:T(8,128)(2,1)S(1)} %terms.1), channel_id=2, replica_groups=mesh['expert'=64,'dp'=8] {'dp'}, dimensions={0}, use_global_device_ids=true | all-gather | bytes 1161216 | tf_op jit(solution)/shard_map/all_gather | solution.py:282
  124.7 0.0 copy-start.9
  124.7 0.0 copy-start.11
  124.7 0.8 scores.1
  125.5 12.9 %all-to-all-start.2 = ((f32[64,1,128]{2,1,0:T(1,128)}), f32[64,1,128]{2,1,0:T(1,128)S(1)}, u32[]{:S(2)}, u32[]{:S(2)}) async-start(f32[64,1,128]{2,1,0:T(1,128)} %scores.1), calls=%async_computation.2 | async-start | bytes 65536 | tf_op jit(solution)/shard_map/all_to_all | solution.py:284
  138.4 0.0 copy-start.2
  138.4 1.2 copy-done.2
  139.5 1.9 %outer.1 = (bf16[1,256,768]{2,1,0:T(8,128)(2,1)}, bf16[1,256,768]{2,1,0:T(8,128)(2,1)}, bf16[1,256,768]{2,1,0:T(8,128)(2,1)}) custom-call(bf16[8,72,896]{2,1,0:T(8,128)(2,1)S(1)} %bitcast.6, bf16[576,768]{1,0:T(8,128)(2,1)S(1)} %get-tuple-element.18.rows_x, bf16[576,768]{1,0:T(8,128)(2,1)S(1)} %copy-done.2), custom_call_target="tpu_custom_call" | custom-call | flops 679477248 | bytes 3538944 | tf_op jit(solution)/shard_map/outer/pallas_call | solution.py:235
  141.4 6.2 %all-to-all-done.2.scores = f32[64,1,128]{2,1,0:T(1,128)S(1)} async-done(((f32[64,1,128]{2,1,0:T(1,128)}), f32[64,1,128]{2,1,0:T(1,128)S(1)}, u32[]{:S(2)}, u32[]{:S(2)}) %all-to-all-start.2) | async-done | bytes 32800 | tf_op jit(solution)/shard_map/all_to_all | solution.py:284
  147.7 0.0 copy-done.9
  147.7 0.0 copy-done.11
  147.7 0.8 place.1
  (1 shorter events, 0.0 us)
Async XLA Ops:
  0.6 1.0 copy-start.6
  1.6 1.0 copy-start.7
  2.6 0.7 copy-start.10
  3.3 0.7 copy-start.12
  5.6 1.3 copy-start
  6.8 0.6 copy-start.8
  7.4 60.4 %copy-start.3 = (bf16[1,256,768]{2,1,0:T(8,128)(2,1)S(1)}, bf16[1,256,768]{2,1,0:T(8,128)(2,1)}, u32[]{:S(2)}) copy-start(bf16[1,256,768]{2,1,0:T(8,128)(2,1)} %w_gate.1) | copy-start | bytes 1179652
  7.4 60.4 %copy-start.4 = (bf16[1,256,768]{2,1,0:T(8,128)(2,1)S(1)}, bf16[1,256,768]{2,1,0:T(8,128)(2,1)}, u32[]{:S(2)}) copy-start(bf16[1,256,768]{2,1,0:T(8,128)(2,1)} %w_up.1) | copy-start | bytes 1179652
  7.4 60.4 %all-to-all-start = ((bf16[64,112,128]{2,1,0:T(8,128)(2,1)}), bf16[64,112,128]{2,1,0:T(8,128)(2,1)S(1)}, u32[]{:S(2)}, u32[]{:S(2)}) async-start(bf16[64,112,128]{2,1,0:T(8,128)(2,1)} %copy-done), calls=%async_computation | async-start | bytes 3670016 | tf_op jit(solution)/shard_map/all_to_all | solution.py:278
  67.8 1.0 copy-start.5
  71.1 0.9 copy-start.1
  124.7 23.0 %copy-start.9 = (f32[64,256]{1,0:T(8,128)S(1)}, f32[64,256]{1,0:T(8,128)}, u32[]{:S(2)}) copy-start(f32[64,256]{1,0:T(8,128)} %copy-done.8) | copy-start | bytes 196612
  124.7 23.0 %copy-start.11 = (s32[256,2]{0,1:T(2,128)S(1)}, s32[256,2]{0,1:T(2,128)}, u32[]{:S(2)}) copy-start(s32[256,2]{0,1:T(2,128)} %param.10) | copy-start | bytes 6148
  125.5 22.1 %all-to-all-start.2 = ((f32[64,1,128]{2,1,0:T(1,128)}), f32[64,1,128]{2,1,0:T(1,128)S(1)}, u32[]{:S(2)}, u32[]{:S(2)}) async-start(f32[64,1,128]{2,1,0:T(1,128)} %scores.1), calls=%async_computation.2 | async-start | bytes 65536 | tf_op jit(solution)/shard_map/all_to_all | solution.py:284
  138.4 1.2 copy-start.2

commit v2 on v1

v2 whole, which is shorter than its diff:
```python
import functools

import jax
import jax.numpy as jnp
from jax import lax
from jax.experimental import pallas as pl
from jax.experimental.pallas import tpu as pltpu
from jax.sharding import PartitionSpec as P

bf16, f32, i32 = jnp.bfloat16, jnp.float32, jnp.int32
LANES, SUB = 128, 8
CAP = 9
LIMIT = 32 * 2**20
WHOLE = 64 * 2**20 - 2**19


def params(limit=LIMIT):
    return pltpu.CompilerParams(vmem_limit_bytes=limit)


def iota(shape, dim):
    return lax.broadcasted_iota(i32, shape, dim)


def mm(a, b, contract=((1,), (0,))):
    return lax.dot_general(a, b, (contract, ((), ())), preferred_element_type=f32)


def copies(pairs, sems):
    return [pltpu.make_async_copy(src, dst, sems.at[i]) for i, (src, dst) in enumerate(pairs)]


def rank_of(routes, experts, toks):
    e = iota((experts, toks), 0)
    first, second = e == routes[0:1, :], e == routes[1:2, :]
    named = first | second
    hot = jnp.where(named, 1.0, 0.0).astype(bf16)
    before = jnp.where(iota((toks, toks), 0) < iota((toks, toks), 1), 1.0, 0.0).astype(bf16)
    return first, second, jnp.where(named, mm(hot, before), -1.0)


def pack_kernel(routes_h, combine_h, tokens_h, grads_h, out_h, routes, combine, tokens, grads, out, last, ins, outs):
    experts = out.shape[0]
    toks, width = tokens.shape
    blocks = width // LANES
    half = blocks * SUB
    arriving = copies(
        [(routes_h, routes), (combine_h, combine), (tokens_h, tokens), (grads_h, grads)], ins
    )
    for c in arriving:
        c.start()
    arriving[0].wait()
    first, second, rank = rank_of(routes, experts, toks)
    slot = iota((experts, SUB, toks), 1)
    spread = jnp.broadcast_to(rank[:, None, :], (experts, SUB, toks))
    pick = jnp.where(spread == slot.astype(f32), 1.0, 0.0)
    pick = pick.reshape(experts * SUB, toks).astype(bf16)
    ninth = jnp.where(rank == float(SUB), 1.0, 0.0).astype(bf16)
    pieces = [slice(0, half), slice(half, 2 * half), slice(2 * half, 2 * half + 2 * SUB)]
    leaving = copies([(out.at[:, p], out_h.at[:, p]) for p in pieces], outs)
    last[...] = jnp.zeros(last.shape, f32)
    for i, source in enumerate((tokens, grads)):
        arriving[2 + i].wait()
        rows = mm(pick, source[...])
        for c in range(blocks):
            tile = rows[:, c * LANES : (c + 1) * LANES].reshape(experts, SUB, LANES)
            at = i * half + c * SUB
            out[:, at : at + SUB, :] = tile.astype(bf16)
        leaving[i].start()
        rows = mm(ninth, source[...])
        for c in range(blocks):
            place = i * blocks + c
            last[place // SUB, pl.ds(place % SUB, experts, stride=SUB), :] = rows[:, c * LANES : (c + 1) * LANES]
    arriving[1].wait()
    prob = combine[...].astype(f32)
    prob = jnp.where(first, prob[0:1, :], jnp.where(second, prob[1:2, :], 0.0))
    lane = iota((experts, LANES), 1)
    row = jnp.zeros((experts, LANES), f32)
    for r in range(CAP):
        value = jnp.sum(jnp.where(rank == float(r), prob, 0.0), axis=1, keepdims=True)
        row = jnp.where(lane == r, value, row)
    place = 2 * blocks
    last[place // SUB, pl.ds(place % SUB, experts, stride=SUB), :] = row
    for k in range(2):
        at = 2 * half + k * SUB
        out[:, at : at + SUB, :] = last[k].reshape(experts, SUB, LANES).astype(bf16)
    leaving[2].start()
    for c in leaving:
        c.wait()


def pack(routes, combine, tokens, grads, experts):
    toks, width = tokens.shape
    shape = (experts, (2 * width // LANES) * SUB + 2 * SUB, LANES)
    args = (routes, combine, tokens, grads)
    return pl.pallas_call(
        pack_kernel,
        in_specs=[pl.BlockSpec(memory_space=pltpu.HBM)] * 4,
        out_specs=pl.BlockSpec(memory_space=pltpu.HBM),
        out_shape=jax.ShapeDtypeStruct(shape, bf16),
        scratch_shapes=[pltpu.VMEM(a.shape, a.dtype) for a in args]
        + [
            pltpu.VMEM(shape, bf16),
            pltpu.VMEM((2, experts * SUB, LANES), f32),
            pltpu.SemaphoreType.DMA((4,)),
            pltpu.SemaphoreType.DMA((3,)),
        ],
        compiler_params=params(WHOLE),
        name="pack",
    )(*args)


def stage_kernel(gate, up, down, out):
    for i, weight in enumerate((gate, up, down)):
        out[i] = weight[0].astype(f32).T.astype(bf16)


def stage(*weights):
    _, hidden, width = weights[0].shape
    return pl.pallas_call(
        stage_kernel,
        out_shape=jax.ShapeDtypeStruct((len(weights), width, hidden), bf16),
        compiler_params=params(),
        cost_estimate=pl.CostEstimate(
            flops=3 * width * hidden, bytes_accessed=12 * width * hidden, transcendentals=0
        ),
        name="stage",
    )(*weights)


def project_kernel(me, recv, weights, part, own, rows_x, rows_dy, probs, last):
    experts = recv.shape[0]
    groups, count, _ = part.shape
    _, width, hidden = weights.shape
    blocks = width // LANES
    main = experts * SUB
    share = main // groups

    def tile(at):
        return recv[:, at : at + SUB, :].astype(f32).reshape(main, LANES)

    for k in range(2):
        last[k] = tile((2 * blocks + k) * SUB)

    def taken(place):
        return last[place // SUB, pl.ds(place % SUB, experts, stride=SUB), :]

    probs[...] = taken(2 * blocks)
    for i, rows in enumerate((rows_x, rows_dy)):
        for c in range(blocks):
            lanes = slice(c * LANES, (c + 1) * LANES)
            rows[0:main, lanes] = tile((i * blocks + c) * SUB).astype(bf16)
            rows[main:, lanes] = taken(i * blocks + c).astype(bf16)
    for i, rows in enumerate((rows_x, rows_x, rows_dy)):
        lanes = slice(i * hidden, (i + 1) * hidden)
        value = mm(rows[...], weights[i])
        for j in range(groups):
            piece = jnp.concatenate(
                [value[j * share : (j + 1) * share], value[main + j * SUB : main + (j + 1) * SUB]]
            )
            part[j, :, lanes] = piece.astype(bf16)

            @pl.when(me[0] == j)
            def _(piece=piece, lanes=lanes):
                own[:, lanes] = piece


def project(me, recv, weights, groups):
    experts = recv.shape[0]
    _, width, hidden = weights.shape
    total = experts * CAP
    count = total // groups
    vmem = pl.BlockSpec(memory_space=pltpu.VMEM)
    return pl.pallas_call(
        project_kernel,
        in_specs=[pl.BlockSpec(memory_space=pltpu.SMEM)] + [vmem] * 2,
        out_shape=(
            jax.ShapeDtypeStruct((groups, count, 3 * hidden), bf16),
            jax.ShapeDtypeStruct((count, 3 * hidden), f32),
            jax.ShapeDtypeStruct((total, width), bf16),
            jax.ShapeDtypeStruct((total, width), bf16),
            jax.ShapeDtypeStruct((experts, LANES), f32),
        ),
        scratch_shapes=[pltpu.VMEM((2, experts * SUB, LANES), f32)],
        compiler_params=params(),
        name="project",
    )(me, recv, weights)


def terms_kernel(me, parts, own, probs, out):
    groups, count, _ = parts.shape
    hidden = parts.shape[2] // 3
    main = count - SUB
    near = probs[pl.ds(pl.multiple_of(me[0] * SUB, SUB), SUB), :]
    lane = iota((SUB, SUB, LANES), 2)
    spread = jnp.broadcast_to(near[:, None, :], (SUB, SUB, LANES))
    picked = jnp.sum(jnp.where(lane == iota((SUB, SUB, LANES), 1), spread, 0.0), axis=2, keepdims=True)
    ninth = jnp.sum(jnp.where(iota((SUB, LANES), 1) == SUB, near, 0.0), axis=1, keepdims=True)
    weight = jnp.concatenate([picked.reshape(main, 1), ninth])

    def total(i):
        lanes = slice(i * hidden, (i + 1) * hidden)
        value = own[:, lanes]
        for j in range(groups):
            value = value + jnp.where(me[0] == j, 0.0, parts[j, :, lanes].astype(f32))
        return value

    gate_pre, up_pre, grad_hid = total(0), total(1), total(2)
    sig = jax.nn.sigmoid(gate_pre)
    silu_out = gate_pre * sig
    inner = silu_out * up_pre
    scaled = weight * grad_hid
    out[:, 0:hidden] = (scaled * up_pre * (sig * (1.0 + gate_pre * (1.0 - sig)))).astype(bf16)
    out[:, hidden : 2 * hidden] = (scaled * silu_out).astype(bf16)
    out[:, 2 * hidden : 3 * hidden] = (weight * inner).astype(bf16)
    score = jnp.sum(inner * grad_hid, axis=1, keepdims=True)
    cube = (SUB, SUB, LANES)
    direct = jnp.broadcast_to(score[:main].reshape(SUB, SUB, 1), cube)
    table = jnp.sum(jnp.where(iota(cube, 2) == iota(cube, 1), direct, 0.0), axis=1)
    table = jnp.where(iota((SUB, LANES), 1) == SUB, score[main:], table)
    high = table.astype(bf16).astype(f32)
    middle = (table - high).astype(bf16).astype(f32)
    low = table - high - middle
    rest = jnp.zeros((count - 3 * SUB, LANES), f32)
    out[:, 3 * hidden :] = jnp.concatenate([high, middle, low, rest]).astype(bf16)


def terms(me, parts, own, probs):
    count, wide = own.shape
    vmem = pl.BlockSpec(memory_space=pltpu.VMEM)
    return pl.pallas_call(
        terms_kernel,
        in_specs=[pl.BlockSpec(memory_space=pltpu.SMEM)] + [vmem] * 3,
        out_shape=jax.ShapeDtypeStruct((count, wide + LANES), bf16),
        compiler_params=params(),
        name="terms",
    )(me, parts, own, probs)


def outer_kernel(routes, rows, rows_x, rows_dy, gate, up, down, ranks):
    groups, count, _ = rows.shape
    hidden = gate.shape[1]
    main = count - SUB
    x, dy = rows_x[...], rows_dy[...]
    for i, (other, out) in enumerate(((x, gate), (x, up), (dy, down))):
        lanes = slice(i * hidden, (i + 1) * hidden)
        direct = rows[:, 0:main, lanes].astype(f32).reshape(groups * main, hidden)
        ninth = rows[:, main:, lanes].astype(f32).reshape(groups * SUB, hidden)
        value = jnp.concatenate([direct, ninth]).astype(bf16)
        out[0] = mm(value, other, ((0,), (0,))).astype(bf16)
    ranks[...] = rank_of(routes, *ranks.shape)[2]


def outer(routes, rows, rows_x, rows_dy, hidden, experts):
    total, width = rows_x.shape
    return pl.pallas_call(
        outer_kernel,
        out_shape=(jax.ShapeDtypeStruct((1, hidden, width), bf16),) * 3
        + (jax.ShapeDtypeStruct((experts, routes.shape[1]), f32),),
        compiler_params=params(),
        cost_estimate=pl.CostEstimate(
            flops=6 * total * width * hidden, bytes_accessed=8 * total * width, transcendentals=0
        ),
        name="outer",
    )(routes, rows, rows_x, rows_dy)


def place_kernel(routes, ranks, scores, out):
    experts, toks = ranks.shape
    rank = ranks[...]
    value = jnp.zeros((experts, toks), f32)
    for r in range(CAP):
        value = jnp.where(rank == float(r), scores[:, r : r + 1], value)
    e = iota((experts, toks), 0)
    for k in range(2):
        out[k : k + 1, :] = jnp.sum(
            jnp.where(e == routes[k : k + 1, :], value, 0.0), axis=0, keepdims=True
        )


def place(routes, ranks, scores):
    return pl.pallas_call(
        place_kernel,
        out_shape=jax.ShapeDtypeStruct(routes.shape, f32),
        compiler_params=params(),
        name="place",
    )(routes, ranks, scores)


def local(tokens, grad_out, combine, routes, w_gate, w_up, w_down):
    experts, groups = lax.axis_size("expert"), lax.axis_size("dp")
    hidden = w_gate.shape[1]
    me = lax.axis_index("dp").astype(i32).reshape(1)
    by_slot = routes.T
    packed = pack(by_slot, combine.T, tokens, grad_out, experts)
    recv = lax.all_to_all(packed, "expert", split_axis=0, concat_axis=0, tiled=True)
    part, own, rows_x, rows_dy, probs = project(me, recv, stage(w_gate, w_up, w_down), groups)
    parts = lax.all_to_all(part, "dp", split_axis=0, concat_axis=0, tiled=True)
    mine = terms(me, parts, own, probs)
    rows = lax.all_gather(mine, "dp", axis=0, tiled=False)
    thirds = rows[:, : 3 * SUB, 3 * hidden :].astype(f32).reshape(groups, 3, SUB, LANES)
    scores = (thirds[:, 0] + thirds[:, 1] + thirds[:, 2]).reshape(experts, 1, LANES)
    returned = lax.all_to_all(scores, "expert", split_axis=0, concat_axis=0, tiled=True)
    *grads, ranks = outer(by_slot, rows, rows_x, rows_dy, hidden, experts)
    return tuple(grads) + (place(by_slot, ranks, returned.reshape(experts, LANES)).T,)


def solution(mesh):
    placed = (
        P("expert", "dp"),
        P("expert", "dp"),
        P("expert", None),
        P("expert", None),
        P("expert", None, "dp"),
        P("expert", None, "dp"),
        P("expert", None, "dp"),
    )
    return jax.shard_map(
        local,
        mesh=mesh,
        in_specs=placed,
        out_specs=(
            P("expert", None, "dp"),
            P("expert", None, "dp"),
            P("expert", None, "dp"),
            P("expert", None),
        ),
        check_vma=False,
    )
```

time: 149 us -> 143 us (0.960)
  local copies, waits for them, and re-layouts: 8.3 us -> 4.33 us
  waiting for transfers between devices: 51.7 us -> 48.1 us
    unnamed x26 -> x16, local copies, waits for them, and re-layouts: 8.28 us -> 4.33 us
    all_to_all x1, waiting for transfers between devices: 45.4 us -> 43 us  [local(): lax.all_to_all(packed, 'expert', split_axis=0, concat_axis=0, tiled=True)]
  transfers between devices with their start and end apart: 2 -> 2, of which waited for: 2 -> 2; matrix products, arithmetic and copies ran while one was open for 0% -> 0% of each run, Pallas kernels for 1% -> 2%
where the time goes in v2:
time: 143 us; the launch traced here: 142 us
  blocking collectives  53 us (37%)
  waiting for transfers between devices  48.1 us (34%)
  starting transfers between devices  27.3 us (19%)
  Pallas kernels  8.35 us (6%)
  local copies, waits for them, and re-layouts  4.33 us (3%)
    all_to_all x1, waiting for transfers between devices, local(): lax.all_to_all(packed, 'expert', split_axis=0, concat_axis=0, tiled=True)  43 us
    all_to_all x1, blocking collectives, local(): parts = lax.all_to_all(part, 'dp', split_axis=0, concat_axis=0, tiled=True)  31.1 us
    all_gather x1, blocking collectives, local(): rows = lax.all_gather(mine, 'dp', axis=0, tiled=False)  21.8 us
    all_to_all x1, starting transfers between devices, local(): lax.all_to_all(packed, 'expert', split_axis=0, concat_axis=0, tiled=True)  15 us
    all_to_all x1, starting transfers between devices, local(): lax.all_to_all(scores, 'expert', split_axis=0, concat_axis=0, tiled=True)  12.4 us
    all_to_all x1, waiting for transfers between devices, local(): lax.all_to_all(scores, 'expert', split_axis=0, concat_axis=0, tiled=True)  5.06 us
    unnamed x16, local copies, waits for them, and re-layouts  4.33 us
    pallas_call x1, Pallas kernels, pack(): pl.pallas_call(pack_kernel, in_specs=[pl.BlockSpec(memory_space=pltpu.HBM...  3.01 us
  transfers between devices with their start and end apart: 2, of which 2 were waited for; matrix products, arithmetic and copies ran while one was open for 0% of the time, Pallas kernels for 2%

profile of v2, /device:TPU:1, one launch (start us, length us, event | category | flops | bytes accessed | tf_op | source)
XLA Modules:
  0.0 142.5 jit_solution(17562180075617390100)
XLA Ops:
  0.6 3.0 %pack.1 = bf16[64,112,128]{2,1,0:T(8,128)(2,1)} custom-call(s32[2,256]{1,0:T(2,128)} %bitcast.15, bf16[2,256]{1,0:T(2,128)(2,1)} %bitcast.19, bf16[256,768]{1,0:T(8,128)(2,1)} %tokens_h.1, bf16[256,768]{1,0:T(8,128)(2,1)} %grads_h.1), custom_call_target="tpu_custom_call" | custom-call | tf_op jit(solution)/shard_map/pack/pallas_call | solution.py:96
  3.6 0.0 copy-start.4
  3.7 15.0 %all-to-all-start = ((bf16[64,112,128]{2,1,0:T(8,128)(2,1)}), bf16[64,112,128]{2,1,0:T(8,128)(2,1)S(1)}, u32[]{:S(2)}, u32[]{:S(2)}) async-start(bf16[64,112,128]{2,1,0:T(8,128)(2,1)} %pack.1), calls=%async_computation | async-start | bytes 3670016 | tf_op jit(solution)/shard_map/all_to_all | solution.py:296
  18.6 0.0 copy-done.4
  18.7 0.0 copy-start.5
  18.7 1.0 copy-done.5
  19.7 0.0 copy-start.6
  19.7 1.0 copy-done.6
  20.7 0.4 stage.1.weights
  21.0 43.0 %all-to-all-done.recv = bf16[64,112,128]{2,1,0:T(8,128)(2,1)S(1)} async-done(((bf16[64,112,128]{2,1,0:T(8,128)(2,1)}), bf16[64,112,128]{2,1,0:T(8,128)(2,1)S(1)}, u32[]{:S(2)}, u32[]{:S(2)}) %all-to-all-start) | async-done | bytes 1835040 | tf_op jit(solution)/shard_map/all_to_all | solution.py:296
  64.1 2.0 %project.1 = (bf16[8,72,768]{2,1,0:T(8,128)(2,1)S(1)}, f32[72,768]{1,0:T(8,128)S(1)}, bf16[576,768]{1,0:T(8,128)(2,1)S(1)}, bf16[576,768]{1,0:T(8,128)(2,1)S(1)}, f32[64,128]{1,0:T(8,128)S(1)}) custom-call(s32[1]{0:T(128)} %bitcast.1.me, bf16[64,112,128]{2,1,0:T(8,128)(2,1)S(1)} %all-to-all-done.recv, bf16[3,768,256]{2,1,0:T(8,128)(2,1)S(1)} %stage.1.weights), custom_call_target="tpu_custom_call" | custom-call | tf_op jit(solution)/shard_map/project/pallas_call | solution.py:174
  66.1 0.0 copy-start
  66.1 0.0 copy-start.2
  66.1 0.0 copy-start.7
  66.1 31.1 %all_to_all.15.parts = bf16[8,72,768]{2,1,0:T(8,128)(2,1)S(1)} all-to-all(bf16[8,72,768]{2,1,0:T(8,128)(2,1)S(1)} %get-tuple-element.13), channel_id=1, replica_groups=mesh['expert'=64,'dp'=8] {'dp'}, dimensions={0} | all-to-all | bytes 1769472 | tf_op jit(solution)/shard_map/all_to_all | solution.py:298
  97.3 0.3 terms.1
  97.6 21.8 %all-gather = bf16[576,896]{1,0:T(8,128)(2,1)S(1)} all-gather(bf16[72,896]{1,0:T(8,128)(2,1)S(1)} %terms.1), channel_id=2, replica_groups=mesh['expert'=64,'dp'=8] {'dp'}, dimensions={0}, use_global_device_ids=true | all-gather | bytes 1161216 | tf_op jit(solution)/shard_map/all_gather | solution.py:300
  119.4 0.0 copy-done
  119.4 0.0 copy-done.2
  119.4 0.6 slice_add_fusion
  120.0 12.4 %all-to-all-start.2 = ((f32[64,1,128]{2,1,0:T(1,128)}), f32[64,1,128]{2,1,0:T(1,128)S(1)}, u32[]{:S(2)}, u32[]{:S(2)}) async-start(f32[64,1,128]{2,1,0:T(1,128)} %bitcast.6), calls=%async_computation.2 | async-start | bytes 65536 | tf_op jit(solution)/shard_map/all_to_all | solution.py:303
  132.4 0.0 copy-done.7
  132.4 0.0 copy-start.1
  132.4 1.2 copy-done.1
  133.6 0.0 copy-start.3
  133.6 1.2 copy-done.3
  134.8 1.9 %outer.1 = (bf16[1,256,768]{2,1,0:T(8,128)(2,1)}, bf16[1,256,768]{2,1,0:T(8,128)(2,1)}, bf16[1,256,768]{2,1,0:T(8,128)(2,1)}, f32[64,256]{1,0:T(8,128)S(1)}) custom-call(s32[2,256]{1,0:T(2,128)S(1)} %bitcast.16, bf16[8,72,896]{2,1,0:T(8,128)(2,1)S(1)} %bitcast.13, bf16[576,768]{1,0:T(8,128)(2,1)S(1)} %copy-done.1, bf16[576,768]{1,0:T(8,128)(2,1)S(1)} %copy-done.3), custom_call_target="tpu_custom_call" | custom-call | flops 679477248 | bytes 3538944 | tf_op jit(solution)/shard_map/outer/pallas_call | solution.py:256
  136.6 5.1 %all-to-all-done.2 = f32[64,1,128]{2,1,0:T(1,128)S(1)} async-done(((f32[64,1,128]{2,1,0:T(1,128)}), f32[64,1,128]{2,1,0:T(1,128)S(1)}, u32[]{:S(2)}, u32[]{:S(2)}) %all-to-all-start.2) | async-done | bytes 32800 | tf_op jit(solution)/shard_map/all_to_all | solution.py:303
  141.7 0.8 place.1
  (1 shorter events, 0.0 us)
Async XLA Ops:
  3.6 15.0 %copy-start.4 = (bf16[1,256,768]{2,1,0:T(8,128)(2,1)S(1)}, bf16[1,256,768]{2,1,0:T(8,128)(2,1)}, u32[]{:S(2)}) copy-start(bf16[1,256,768]{2,1,0:T(8,128)(2,1)} %gate.1) | copy-start | bytes 1179652
  3.7 60.4 %all-to-all-start = ((bf16[64,112,128]{2,1,0:T(8,128)(2,1)}), bf16[64,112,128]{2,1,0:T(8,128)(2,1)S(1)}, u32[]{:S(2)}, u32[]{:S(2)}) async-start(bf16[64,112,128]{2,1,0:T(8,128)(2,1)} %pack.1), calls=%async_computation | async-start | bytes 3670016 | tf_op jit(solution)/shard_map/all_to_all | solution.py:296
  18.7 1.0 copy-start.5
  19.7 1.0 copy-start.6
  66.1 53.3 %copy-start = (bf16[576,768]{1,0:T(8,128)(2,1)}, bf16[576,768]{1,0:T(8,128)(2,1)S(1)}, u32[]{:S(2)}) copy-start(bf16[576,768]{1,0:T(8,128)(2,1)S(1)} %get-tuple-element.16.rows_x) | copy-start | bytes 2654212
  66.1 53.3 %copy-start.2 = (bf16[576,768]{1,0:T(8,128)(2,1)}, bf16[576,768]{1,0:T(8,128)(2,1)S(1)}, u32[]{:S(2)}) copy-start(bf16[576,768]{1,0:T(8,128)(2,1)S(1)} %get-tuple-element.17.rows_dy) | copy-start | bytes 2654212
  66.1 66.3 %copy-start.7 = (s32[256,2]{0,1:T(2,128)S(1)}, s32[256,2]{0,1:T(2,128)}, u32[]{:S(2)}) copy-start(s32[256,2]{0,1:T(2,128)} %param.10) | copy-start | bytes 6148
  120.0 21.7 %all-to-all-start.2 = ((f32[64,1,128]{2,1,0:T(1,128)}), f32[64,1,128]{2,1,0:T(1,128)S(1)}, u32[]{:S(2)}, u32[]{:S(2)}) async-start(f32[64,1,128]{2,1,0:T(1,128)} %bitcast.6), calls=%async_computation.2 | async-start | bytes 65536 | tf_op jit(solution)/shard_map/all_to_all | solution.py:303
  132.4 1.2 copy-start.1
  133.6 1.2 copy-start.3

commit v3 on v2

--- a/solution.py
+++ b/solution.py
@@ -9,6 +9,7 @@
 
 bf16, f32, i32 = jnp.bfloat16, jnp.float32, jnp.int32
 LANES, SUB = 128, 8
+TERM = 16
 CAP = 9
 LIMIT = 32 * 2**20
 WHOLE = 64 * 2**20 - 2**19
@@ -210,44 +211,59 @@
     silu_out = gate_pre * sig
     inner = silu_out * up_pre
     scaled = weight * grad_hid
-    out[:, 0:hidden] = (scaled * up_pre * (sig * (1.0 + gate_pre * (1.0 - sig)))).astype(bf16)
-    out[:, hidden : 2 * hidden] = (scaled * silu_out).astype(bf16)
-    out[:, 2 * hidden : 3 * hidden] = (weight * inner).astype(bf16)
+    rows = (
+        scaled * up_pre * (sig * (1.0 + gate_pre * (1.0 - sig))),
+        scaled * silu_out,
+        weight * inner,
+    )
+    per = hidden // LANES
+    for i in range(3 * per):
+        block = rows[i // per][:, i % per * LANES : (i % per + 1) * LANES].astype(bf16)
+        for j in range(out.shape[0]):
+            out[j, i * count : (i + 1) * count, :] = block
     score = jnp.sum(inner * grad_hid, axis=1, keepdims=True)
     cube = (SUB, SUB, LANES)
+    lane = iota(cube, 2)
     direct = jnp.broadcast_to(score[:main].reshape(SUB, SUB, 1), cube)
-    table = jnp.sum(jnp.where(iota(cube, 2) == iota(cube, 1), direct, 0.0), axis=1)
-    table = jnp.where(iota((SUB, LANES), 1) == SUB, score[main:], table)
+    table = jnp.sum(jnp.where(lane % TERM == iota(cube, 1), direct, 0.0), axis=1)
+    lane = iota((SUB, LANES), 1)
+    table = jnp.where(lane % TERM == SUB, score[main:], table)
     high = table.astype(bf16).astype(f32)
     middle = (table - high).astype(bf16).astype(f32)
     low = table - high - middle
-    rest = jnp.zeros((count - 3 * SUB, LANES), f32)
-    out[:, 3 * hidden :] = jnp.concatenate([high, middle, low, rest]).astype(bf16)
-
-
-def terms(me, parts, own, probs):
+    table = jnp.where(lane < TERM, high, jnp.where(lane < 2 * TERM, middle, low))
+    for j in range(out.shape[0]):
+        out[j, 3 * per * count :, :] = table.astype(bf16)
+
+
+def terms(me, parts, own, probs, times):
     count, wide = own.shape
     vmem = pl.BlockSpec(memory_space=pltpu.VMEM)
     return pl.pallas_call(
         terms_kernel,
         in_specs=[pl.BlockSpec(memory_space=pltpu.SMEM)] + [vmem] * 3,
-        out_shape=jax.ShapeDtypeStruct((count, wide + LANES), bf16),
+        out_shape=jax.ShapeDtypeStruct((times, count * wide // LANES + SUB, LANES), bf16),
         compiler_params=params(),
         name="terms",
     )(me, parts, own, probs)
 
 
 def outer_kernel(routes, rows, rows_x, rows_dy, gate, up, down, ranks):
-    groups, count, _ = rows.shape
+    groups = rows.shape[0]
     hidden = gate.shape[1]
+    per = hidden // LANES
+    count = (rows.shape[1] - SUB) // (3 * per)
     main = count - SUB
-    x, dy = rows_x[...], rows_dy[...]
-    for i, (other, out) in enumerate(((x, gate), (x, up), (dy, down))):
-        lanes = slice(i * hidden, (i + 1) * hidden)
-        direct = rows[:, 0:main, lanes].astype(f32).reshape(groups * main, hidden)
-        ninth = rows[:, main:, lanes].astype(f32).reshape(groups * SUB, hidden)
-        value = jnp.concatenate([direct, ninth]).astype(bf16)
-        out[0] = mm(value, other, ((0,), (0,))).astype(bf16)
+
+    def block(i):
+        at = i * count
+        direct = rows[:, at : at + main, :].astype(f32).reshape(groups * main, LANES)
+        ninth = rows[:, at + main : at + count, :].astype(f32).reshape(groups * SUB, LANES)
+        return jnp.concatenate([direct, ninth]).astype(bf16)
+
+    for i, (other, out) in enumerate(((rows_x, gate), (rows_x, up), (rows_dy, down))):
+        value = jnp.concatenate([block(i * per + c) for c in range(per)], axis=1)
+        out[0] = mm(value, other[...], ((0,), (0,))).astype(bf16)
     ranks[...] = rank_of(routes, *ranks.shape)[2]
 
 
@@ -268,9 +284,10 @@
 def place_kernel(routes, ranks, scores, out):
     experts, toks = ranks.shape
     rank = ranks[...]
+    table = scores[:, 0:TERM] + scores[:, TERM : 2 * TERM] + scores[:, 2 * TERM : 3 * TERM]
     value = jnp.zeros((experts, toks), f32)
     for r in range(CAP):
-        value = jnp.where(rank == float(r), scores[:, r : r + 1], value)
+        value = jnp.where(rank == float(r), table[:, r : r + 1], value)
     e = iota((experts, toks), 0)
     for k in range(2):
         out[k : k + 1, :] = jnp.sum(
@@ -290,16 +307,33 @@
 def local(tokens, grad_out, combine, routes, w_gate, w_up, w_down):
     experts, groups = lax.axis_size("expert"), lax.axis_size("dp")
     hidden = w_gate.shape[1]
-    me = lax.axis_index("dp").astype(i32).reshape(1)
+    y, core = lax.axis_index("dp").astype(i32), lax.axis_index("expert").astype(i32) & 1
+    me = jnp.where(core == 1, groups - 1 - y, y).reshape(1)
     by_slot = routes.T
     packed = pack(by_slot, combine.T, tokens, grad_out, experts)
     recv = lax.all_to_all(packed, "expert", split_axis=0, concat_axis=0, tiled=True)
     part, own, rows_x, rows_dy, probs = project(me, recv, stage(w_gate, w_up, w_down), groups)
-    parts = lax.all_to_all(part, "dp", split_axis=0, concat_axis=0, tiled=True)
-    mine = terms(me, parts, own, probs)
-    rows = lax.all_gather(mine, "dp", axis=0, tiled=False)
-    thirds = rows[:, : 3 * SUB, 3 * hidden :].astype(f32).reshape(groups, 3, SUB, LANES)
-    scores = (thirds[:, 0] + thirds[:, 1] + thirds[:, 2]).reshape(experts, 1, LANES)
+    both = ("expert", "dp")
+    lines = [
+        [e * groups + (groups - 1 - j if e % 2 else j) for j in range(groups)] for e in range(experts)
+    ]
+
+    def exchange(pieces):
+        return lax.all_to_all(
+            pieces, both, split_axis=0, concat_axis=0, tiled=True, axis_index_groups=lines
+        )
+
+    def by_source(rows):
+        return rows, rows[:, -SUB:, :].astype(f32).reshape(experts, 1, LANES)
+
+    def even(part, own, probs):
+        return by_source(exchange(terms(me, exchange(part), own, probs, groups)))
+
+    def odd(part, own, probs):
+        mine = terms(me, exchange(part), own, probs, 1)
+        return by_source(lax.all_gather(mine, both, axis=0, tiled=True, axis_index_groups=lines))
+
+    rows, scores = lax.cond(core == 0, even, odd, part, own, probs)
     returned = lax.all_to_all(scores, "expert", split_axis=0, concat_axis=0, tiled=True)
     *grads, ranks = outer(by_slot, rows, rows_x, rows_dy, hidden, experts)
     return tuple(grads) + (place(by_slot, ranks, returned.reshape(experts, LANES)).T,)

time: 143 us -> 139 us (0.972)
  starting transfers between devices: 27.3 us -> 21.7 us
  waiting for transfers between devices: 48.1 us -> 50.4 us
    all_to_all x1, starting transfers between devices: 12.4 us -> 6.73 us  [local(): lax.all_to_all(scores, 'expert', split_axis=0, concat_axis=0, tiled=True)]
    all_gather x1, blocking collectives: 21.8 us -> 26.1 us  [odd(): lax.all_gather(mine, both, axis=0, tiled=True, axis_index_groups=lines)]
    all_to_all x1, blocking collectives: 31.1 us -> 26.9 us  [exchange(): lax.all_to_all(pieces, both, split_axis=0, concat_axis=0, tiled=True, axi...]
    all_to_all x1, waiting for transfers between devices: 5.06 us -> 7.37 us  [local(): lax.all_to_all(scores, 'expert', split_axis=0, concat_axis=0, tiled=True)]
where the time goes in v3:
time: 139 us
  blocking collectives  53 us (38%)
  waiting for transfers between devices  50.4 us (36%)
  starting transfers between devices  21.7 us (16%)
  Pallas kernels  8.48 us (6%)
  local copies, waits for them, and re-layouts  3.87 us (3%)
    all_to_all x1, waiting for transfers between devices, local(): lax.all_to_all(packed, 'expert', split_axis=0, concat_axis=0, tiled=True)  43 us
    all_to_all x1, blocking collectives, exchange(): lax.all_to_all(pieces, both, split_axis=0, concat_axis=0, tiled=True, axi...  26.9 us
    all_gather x1, blocking collectives, odd(): lax.all_gather(mine, both, axis=0, tiled=True, axis_index_groups=lines)  26.1 us
    all_to_all x1, starting transfers between devices, local(): lax.all_to_all(packed, 'expert', split_axis=0, concat_axis=0, tiled=True)  15 us
    all_to_all x1, waiting for transfers between devices, local(): lax.all_to_all(scores, 'expert', split_axis=0, concat_axis=0, tiled=True)  7.37 us
    all_to_all x1, starting transfers between devices, local(): lax.all_to_all(scores, 'expert', split_axis=0, concat_axis=0, tiled=True)  6.73 us
    unnamed x16, local copies, waits for them, and re-layouts  3.87 us
    pallas_call x1, Pallas kernels, pack(): pl.pallas_call(pack_kernel, in_specs=[pl.BlockSpec(memory_space=pltpu.HBM...  3.06 us
  transfers between devices with their start and end apart: 2, of which 2 were waited for; matrix products, arithmetic and copies ran while one was open for 0% of the time, Pallas kernels for 2%

profile of v3, /device:TPU:1, one launch (start us, length us, event | category | flops | bytes accessed | tf_op | source)
XLA Modules:
  0.0 138.8 jit_solution(2851719188144502518)
XLA Ops:
  0.6 3.1 %pack.1 = bf16[64,112,128]{2,1,0:T(8,128)(2,1)} custom-call(s32[2,256]{1,0:T(2,128)} %bitcast.7, bf16[2,256]{1,0:T(2,128)(2,1)} %bitcast.11, bf16[256,768]{1,0:T(8,128)(2,1)} %tokens_h.1, bf16[256,768]{1,0:T(8,128)(2,1)} %grads_h.1), custom_call_target="tpu_custom_call" | custom-call | tf_op jit(solution)/shard_map/pack/pallas_call | solution.py:97
  3.7 0.0 copy-start.4
  3.7 15.0 %all-to-all-start.3 = ((bf16[64,112,128]{2,1,0:T(8,128)(2,1)}), bf16[64,112,128]{2,1,0:T(8,128)(2,1)S(1)}, u32[]{:S(2)}, u32[]{:S(2)}) async-start(bf16[64,112,128]{2,1,0:T(8,128)(2,1)} %pack.1), calls=%async_computation.3 | async-start | bytes 3670016 | tf_op jit(solution)/shard_map/all_to_all | solution.py:314
  18.7 0.0 copy-done.4
  18.7 0.0 copy-start.5
  18.7 1.0 copy-done.5
  19.7 0.0 copy-start.6
  19.7 1.0 copy-done.6
  20.7 0.4 stage.1.weights
  21.1 43.0 %all-to-all-done.3.recv = bf16[64,112,128]{2,1,0:T(8,128)(2,1)S(1)} async-done(((bf16[64,112,128]{2,1,0:T(8,128)(2,1)}), bf16[64,112,128]{2,1,0:T(8,128)(2,1)S(1)}, u32[]{:S(2)}, u32[]{:S(2)}) %all-to-all-start.3) | async-done | bytes 1835040 | tf_op jit(solution)/shard_map/all_to_all | solution.py:314
  64.1 2.0 %project.1 = (bf16[8,72,768]{2,1,0:T(8,128)(2,1)S(1)}, f32[72,768]{1,0:T(8,128)S(1)}, bf16[576,768]{1,0:T(8,128)(2,1)S(1)}, bf16[576,768]{1,0:T(8,128)(2,1)S(1)}, f32[64,128]{1,0:T(8,128)S(1)}) custom-call(s32[1]{0:T(128)} %bitcast.1.me, bf16[64,112,128]{2,1,0:T(8,128)(2,1)S(1)} %all-to-all-done.3.recv, bf16[3,768,256]{2,1,0:T(8,128)(2,1)S(1)} %stage.1.weights), custom_call_target="tpu_custom_call" | custom-call | tf_op jit(solution)/shard_map/project/pallas_call | solution.py:175
  66.2 0.0 copy-start
  66.2 0.9 copy-done
  67.1 0.0 copy-start.2
  67.1 1.0 copy-done.2
  68.0 0.0 copy-start.1
  68.0 0.0 copy-start.3
  68.0 0.0 copy-start.7
  68.0 53.3 %conditional.2 = (bf16[8,440,128]{2,1,0:T(8,128)(2,1)S(1)}) conditional(s32[]{:T(128)} %convert_element_type.6, (bf16[8,72,768]{2,1,0:T(8,128)(2,1)S(1)}, s32[1]{0:T(128)}, f32[72,768]{1,0:T(8,128)S(1)}, f32[64,128]{1,0:T(8,128)S(1)}) %tuple.23, (bf16[8,72,768]{2,1,0:T(8,128)(2,1)S(1)}, s32[1]{0:T(128)}, f32[72,768]{1,0:T(8,128)S(1)}, ...), branch_computations={%region_0.1_spmd, %region_1.2_spmd} | conditional | bytes 3571720
  68.0 26.9 %all_to_all.22.parts = bf16[8,72,768]{2,1,0:T(8,128)(2,1)S(1)} all-to-all(bf16[8,72,768]{2,1,0:T(8,128)(2,1)S(1)} %get-tuple-element.25), channel_id=1, replica_groups={{0,1,2,3,4,5,6,7},{15,14,13,12,11,10,9,8},{16,17,18,19,20,21,22,23},{31..., dimensions={0} | all-to-all | bytes 1769472 | tf_op jit(solution)/shard_map/cond/branch_0_fun/all_to_all | solution.py:322
  95.0 0.3 terms.2
  95.3 26.1 %all_gather.2 = bf16[8,440,128]{2,1,0:T(8,128)(2,1)S(1)} all-gather(bf16[1,440,128]{2,1,0:T(8,128)(2,1)S(1)} %terms.2), channel_id=1, replica_groups={{0,1,2,3,4,5,6,7},{15,14,13,12,11,10,9,8},{16,17,18,19,20,21,22,23},{31..., dimensions={0}, use_global_device_ids=true | all-gather | bytes 1013760 | tf_op jit(solution)/shard_map/cond/branch_0_fun/all_gather | solution.py:334
  121.3 0.6 slice_convert_fusion
  122.0 6.7 %all-to-all-start.4 = ((f32[64,1,128]{2,1,0:T(1,128)}), f32[64,1,128]{2,1,0:T(1,128)S(1)}, u32[]{:S(2)}, u32[]{:S(2)}) async-start(f32[64,1,128]{2,1,0:T(1,128)} %bitcast.3), calls=%async_computation.4 | async-start | bytes 65536 | tf_op jit(solution)/shard_map/all_to_all | solution.py:337
  128.7 0.0 copy-done.1
  128.7 0.0 copy-done.3
  128.7 0.0 copy-done.7
  128.7 1.9 %outer.1 = (bf16[1,256,768]{2,1,0:T(8,128)(2,1)}, bf16[1,256,768]{2,1,0:T(8,128)(2,1)}, bf16[1,256,768]{2,1,0:T(8,128)(2,1)}, f32[64,256]{1,0:T(8,128)S(1)}) custom-call(s32[2,256]{1,0:T(2,128)S(1)} %bitcast.8, bf16[8,440,128]{2,1,0:T(8,128)(2,1)S(1)} %get-tuple-element.54.rows, bf16[576,768]{1,0:T(8,128)(2,1)S(1)} %copy-done.1, bf16[576,768]{1,0:T(8,128)(2,1)S(1)} %copy-done.3), custom_call_target="tpu_custom_call" | custom-call | flops 679477248 | bytes 3538944 | tf_op jit(solution)/shard_map/outer/pallas_call | solution.py:272
  130.6 7.4 %all-to-all-done.4 = f32[64,1,128]{2,1,0:T(1,128)S(1)} async-done(((f32[64,1,128]{2,1,0:T(1,128)}), f32[64,1,128]{2,1,0:T(1,128)S(1)}, u32[]{:S(2)}, u32[]{:S(2)}) %all-to-all-start.4) | async-done | bytes 32800 | tf_op jit(solution)/shard_map/all_to_all | solution.py:337
  138.0 0.8 place.1
Async XLA Ops:
  3.7 15.0 %copy-start.4 = (bf16[1,256,768]{2,1,0:T(8,128)(2,1)S(1)}, bf16[1,256,768]{2,1,0:T(8,128)(2,1)}, u32[]{:S(2)}) copy-start(bf16[1,256,768]{2,1,0:T(8,128)(2,1)} %gate.1) | copy-start | bytes 1179652
  3.7 60.4 %all-to-all-start.3 = ((bf16[64,112,128]{2,1,0:T(8,128)(2,1)}), bf16[64,112,128]{2,1,0:T(8,128)(2,1)S(1)}, u32[]{:S(2)}, u32[]{:S(2)}) async-start(bf16[64,112,128]{2,1,0:T(8,128)(2,1)} %pack.1), calls=%async_computation.3 | async-start | bytes 3670016 | tf_op jit(solution)/shard_map/all_to_all | solution.py:314
  18.7 1.0 copy-start.5
  19.7 1.0 copy-start.6
  66.2 0.9 copy-start
  67.1 1.0 copy-start.2
  68.0 60.7 %copy-start.1 = (bf16[576,768]{1,0:T(8,128)(2,1)S(1)}, bf16[576,768]{1,0:T(8,128)(2,1)}, u32[]{:S(2)}) copy-start(bf16[576,768]{1,0:T(8,128)(2,1)} %copy-done) | copy-start | bytes 2654212
  68.0 60.7 %copy-start.3 = (bf16[576,768]{1,0:T(8,128)(2,1)S(1)}, bf16[576,768]{1,0:T(8,128)(2,1)}, u32[]{:S(2)}) copy-start(bf16[576,768]{1,0:T(8,128)(2,1)} %copy-done.2) | copy-start | bytes 2654212
  68.0 60.7 %copy-start.7 = (s32[256,2]{0,1:T(2,128)S(1)}, s32[256,2]{0,1:T(2,128)}, u32[]{:S(2)}) copy-start(s32[256,2]{0,1:T(2,128)} %param.12) | copy-start | bytes 6148
  122.0 16.0 %all-to-all-start.4 = ((f32[64,1,128]{2,1,0:T(1,128)}), f32[64,1,128]{2,1,0:T(1,128)S(1)}, u32[]{:S(2)}, u32[]{:S(2)}) async-start(f32[64,1,128]{2,1,0:T(1,128)} %bitcast.3), calls=%async_computation.4 | async-start | bytes 65536 | tf_op jit(solution)/shard_map/all_to_all | solution.py:337

commit v4 on v3

--- a/solution.py
+++ b/solution.py
@@ -10,6 +10,7 @@
 bf16, f32, i32 = jnp.bfloat16, jnp.float32, jnp.int32
 LANES, SUB = 128, 8
 TERM = 16
+TURN = 5
 CAP = 9
 LIMIT = 32 * 2**20
 WHOLE = 64 * 2**20 - 2**19
@@ -129,13 +130,10 @@
     )(*weights)
 
 
-def project_kernel(me, recv, weights, part, own, rows_x, rows_dy, probs, last):
+def unpack(recv, rows_x, rows_dy, last):
     experts = recv.shape[0]
-    groups, count, _ = part.shape
-    _, width, hidden = weights.shape
-    blocks = width // LANES
+    blocks = rows_x.shape[1] // LANES
     main = experts * SUB
-    share = main // groups
 
     def tile(at):
         return recv[:, at : at + SUB, :].astype(f32).reshape(main, LANES)
@@ -146,12 +144,20 @@
     def taken(place):
         return last[place // SUB, pl.ds(place % SUB, experts, stride=SUB), :]
 
-    probs[...] = taken(2 * blocks)
     for i, rows in enumerate((rows_x, rows_dy)):
         for c in range(blocks):
             lanes = slice(c * LANES, (c + 1) * LANES)
             rows[0:main, lanes] = tile((i * blocks + c) * SUB).astype(bf16)
             rows[main:, lanes] = taken(i * blocks + c).astype(bf16)
+    return taken(2 * blocks)
+
+
+def project_kernel(me, recv, weights, part, own, probs, rows_x, rows_dy, last):
+    groups = part.shape[0]
+    _, width, hidden = weights.shape
+    main = recv.shape[0] * SUB
+    share = main // groups
+    probs[...] = unpack(recv, rows_x, rows_dy, last)
     for i, rows in enumerate((rows_x, rows_x, rows_dy)):
         lanes = slice(i * hidden, (i + 1) * hidden)
         value = mm(rows[...], weights[i])
@@ -166,6 +172,11 @@
                 own[:, lanes] = piece
 
 
+def unpacked(experts, width):
+    rows = pltpu.VMEM((experts * CAP, width), bf16)
+    return [rows, rows, pltpu.VMEM((2, experts * SUB, LANES), f32)]
+
+
 def project(me, recv, weights, groups):
     experts = recv.shape[0]
     _, width, hidden = weights.shape
@@ -178,11 +189,9 @@
         out_shape=(
             jax.ShapeDtypeStruct((groups, count, 3 * hidden), bf16),
             jax.ShapeDtypeStruct((count, 3 * hidden), f32),
-            jax.ShapeDtypeStruct((total, width), bf16),
-            jax.ShapeDtypeStruct((total, width), bf16),
             jax.ShapeDtypeStruct((experts, LANES), f32),
         ),
-        scratch_shapes=[pltpu.VMEM((2, experts * SUB, LANES), f32)],
+        scratch_shapes=unpacked(experts, width),
         compiler_params=params(),
         name="project",
     )(me, recv, weights)
@@ -248,12 +257,13 @@
     )(me, parts, own, probs)
 
 
-def outer_kernel(routes, rows, rows_x, rows_dy, gate, up, down, ranks):
+def outer_kernel(routes, rows, recv, gate, up, down, ranks, rows_x, rows_dy, last):
     groups = rows.shape[0]
     hidden = gate.shape[1]
     per = hidden // LANES
     count = (rows.shape[1] - SUB) // (3 * per)
     main = count - SUB
+    unpack(recv, rows_x, rows_dy, last)
 
     def block(i):
         at = i * count
@@ -267,18 +277,20 @@
     ranks[...] = rank_of(routes, *ranks.shape)[2]
 
 
-def outer(routes, rows, rows_x, rows_dy, hidden, experts):
-    total, width = rows_x.shape
+def outer(routes, rows, recv, hidden, width):
+    experts = recv.shape[0]
+    total = experts * CAP
     return pl.pallas_call(
         outer_kernel,
         out_shape=(jax.ShapeDtypeStruct((1, hidden, width), bf16),) * 3
         + (jax.ShapeDtypeStruct((experts, routes.shape[1]), f32),),
+        scratch_shapes=unpacked(experts, width),
         compiler_params=params(),
         cost_estimate=pl.CostEstimate(
             flops=6 * total * width * hidden, bytes_accessed=8 * total * width, transcendentals=0
         ),
         name="outer",
-    )(routes, rows, rows_x, rows_dy)
+    )(routes, rows, recv)
 
 
 def place_kernel(routes, ranks, scores, out):
@@ -308,14 +320,14 @@
     experts, groups = lax.axis_size("expert"), lax.axis_size("dp")
     hidden = w_gate.shape[1]
     y, core = lax.axis_index("dp").astype(i32), lax.axis_index("expert").astype(i32) & 1
-    me = jnp.where(core == 1, groups - 1 - y, y).reshape(1)
+    me = jnp.where(core == 1, lax.rem(TURN + groups - y, groups), y).reshape(1)
     by_slot = routes.T
     packed = pack(by_slot, combine.T, tokens, grad_out, experts)
     recv = lax.all_to_all(packed, "expert", split_axis=0, concat_axis=0, tiled=True)
-    part, own, rows_x, rows_dy, probs = project(me, recv, stage(w_gate, w_up, w_down), groups)
+    part, own, probs = project(me, recv, stage(w_gate, w_up, w_down), groups)
     both = ("expert", "dp")
     lines = [
-        [e * groups + (groups - 1 - j if e % 2 else j) for j in range(groups)] for e in range(experts)
+        [e * groups + ((TURN - j) % groups if e % 2 else j) for j in range(groups)] for e in range(experts)
     ]
 
     def exchange(pieces):
@@ -335,7 +347,7 @@
 
     rows, scores = lax.cond(core == 0, even, odd, part, own, probs)
     returned = lax.all_to_all(scores, "expert", split_axis=0, concat_axis=0, tiled=True)
-    *grads, ranks = outer(by_slot, rows, rows_x, rows_dy, hidden, experts)
+    *grads, ranks = outer(by_slot, rows, recv, hidden, tokens.shape[1])
     return tuple(grads) + (place(by_slot, ranks, returned.reshape(experts, LANES)).T,)
 
 

time: 139 us -> 137 us (0.986)
  local copies, waits for them, and re-layouts: 3.87 us -> 2 us
    unnamed x16 -> x8, local copies, waits for them, and re-layouts: 3.87 us -> 2 us
    all_gather x1, blocking collectives: 26.1 us -> 24.6 us  [odd(): lax.all_gather(mine, both, axis=0, tiled=True, axis_index_groups=lines)]
where the time goes in v4:
time: 137 us; the launch traced here: 136 us
  blocking collectives  51.7 us (38%)
  waiting for transfers between devices  50.3 us (37%)
  starting transfers between devices  22.2 us (16%)
  Pallas kernels  8.53 us (6%)
  local copies, waits for them, and re-layouts  2 us (1%)
    all_to_all x1, waiting for transfers between devices, local(): lax.all_to_all(packed, 'expert', split_axis=0, concat_axis=0, tiled=True)  43 us
    all_to_all x1, blocking collectives, exchange(): lax.all_to_all(pieces, both, split_axis=0, concat_axis=0, tiled=True, axi...  27.1 us
    all_gather x1, blocking collectives, odd(): lax.all_gather(mine, both, axis=0, tiled=True, axis_index_groups=lines)  24.6 us
    all_to_all x1, starting transfers between devices, local(): lax.all_to_all(packed, 'expert', split_axis=0, concat_axis=0, tiled=True)  15 us
    all_to_all x1, waiting for transfers between devices, local(): lax.all_to_all(scores, 'expert', split_axis=0, concat_axis=0, tiled=True)  7.32 us
    all_to_all x1, starting transfers between devices, local(): lax.all_to_all(scores, 'expert', split_axis=0, concat_axis=0, tiled=True)  7.18 us
    pallas_call x1, Pallas kernels, pack(): pl.pallas_call(pack_kernel, in_specs=[pl.BlockSpec(memory_space=pltpu.HBM...  3.04 us
  transfers between devices with their start and end apart: 2, of which 2 were waited for; matrix products, arithmetic and copies ran while one was open for 0% of the time, Pallas kernels for 2%

profile of v4, /device:TPU:1, one launch (start us, length us, event | category | flops | bytes accessed | tf_op | source)
XLA Modules:
  0.0 136.1 jit_solution(1840777533100890792)
XLA Ops:
  0.6 3.0 %pack.1 = bf16[64,112,128]{2,1,0:T(8,128)(2,1)} custom-call(s32[2,256]{1,0:T(2,128)} %bitcast.7, bf16[2,256]{1,0:T(2,128)(2,1)} %bitcast.11, bf16[256,768]{1,0:T(8,128)(2,1)} %tokens_h.1, bf16[256,768]{1,0:T(8,128)(2,1)} %grads_h.1), custom_call_target="tpu_custom_call" | custom-call | tf_op jit(solution)/shard_map/pack/pallas_call | solution.py:98
  3.7 0.0 copy-start
  3.7 15.0 %all-to-all-start.3 = ((bf16[64,112,128]{2,1,0:T(8,128)(2,1)}), bf16[64,112,128]{2,1,0:T(8,128)(2,1)S(1)}, u32[]{:S(2)}, u32[]{:S(2)}) async-start(bf16[64,112,128]{2,1,0:T(8,128)(2,1)} %pack.1), calls=%async_computation.3 | async-start | bytes 3670016 | tf_op jit(solution)/shard_map/all_to_all | solution.py:326
  18.7 0.0 copy-done
  18.7 0.0 copy-start.1
  18.7 1.0 copy-done.1
  19.7 0.0 copy-start.2
  19.7 1.0 copy-done.2
  20.7 0.4 stage.1.weights
  21.1 43.0 %all-to-all-done.3.recv = bf16[64,112,128]{2,1,0:T(8,128)(2,1)S(1)} async-done(((bf16[64,112,128]{2,1,0:T(8,128)(2,1)}), bf16[64,112,128]{2,1,0:T(8,128)(2,1)S(1)}, u32[]{:S(2)}, u32[]{:S(2)}) %all-to-all-start.3) | async-done | bytes 1835040 | tf_op jit(solution)/shard_map/all_to_all | solution.py:326
  64.1 2.0 %project.1 = (bf16[8,72,768]{2,1,0:T(8,128)(2,1)S(1)}, f32[72,768]{1,0:T(8,128)S(1)}, f32[64,128]{1,0:T(8,128)S(1)}) custom-call(s32[1]{0:T(128)} %bitcast.1.me, bf16[64,112,128]{2,1,0:T(8,128)(2,1)S(1)} %all-to-all-done.3.recv, bf16[3,768,256]{2,1,0:T(8,128)(2,1)S(1)} %stage.1.weights), custom_call_target="tpu_custom_call" | custom-call | tf_op jit(solution)/shard_map/project/pallas_call | solution.py:186
  66.1 0.0 copy-start.3
  66.1 52.0 %conditional.2 = (bf16[8,440,128]{2,1,0:T(8,128)(2,1)S(1)}) conditional(s32[]{:T(128)} %convert_element_type.6, (bf16[8,72,768]{2,1,0:T(8,128)(2,1)S(1)}, s32[1]{0:T(128)}, f32[72,768]{1,0:T(8,128)S(1)}, f32[64,128]{1,0:T(8,128)S(1)}) %tuple.23, (bf16[8,72,768]{2,1,0:T(8,128)(2,1)S(1)}, s32[1]{0:T(128)}, f32[72,768]{1,0:T(8,128)S(1)}, ...), branch_computations={%region_0.1_spmd, %region_1.2_spmd} | conditional | bytes 3571720
  66.2 27.1 %all_to_all.22.parts = bf16[8,72,768]{2,1,0:T(8,128)(2,1)S(1)} all-to-all(bf16[8,72,768]{2,1,0:T(8,128)(2,1)S(1)} %get-tuple-element.25), channel_id=1, replica_groups={{0,1,2,3,4,5,6,7},{13,12,11,10,9,8,15,14},{16,17,18,19,20,21,22,23},{29..., dimensions={0} | all-to-all | bytes 1769472 | tf_op jit(solution)/shard_map/cond/branch_0_fun/all_to_all | solution.py:334
  93.2 0.3 terms.2
  93.5 24.6 %all_gather.2 = bf16[8,440,128]{2,1,0:T(8,128)(2,1)S(1)} all-gather(bf16[1,440,128]{2,1,0:T(8,128)(2,1)S(1)} %terms.2), channel_id=1, replica_groups={{0,1,2,3,4,5,6,7},{13,12,11,10,9,8,15,14},{16,17,18,19,20,21,22,23},{29..., dimensions={0}, use_global_device_ids=true | all-gather | bytes 1013760 | tf_op jit(solution)/shard_map/cond/branch_0_fun/all_gather | solution.py:346
  118.2 0.6 slice_convert_fusion
  118.8 7.2 %all-to-all-start.4 = ((f32[64,1,128]{2,1,0:T(1,128)}), f32[64,1,128]{2,1,0:T(1,128)S(1)}, u32[]{:S(2)}, u32[]{:S(2)}) async-start(f32[64,1,128]{2,1,0:T(1,128)} %bitcast.3), calls=%async_computation.4 | async-start | bytes 65536 | tf_op jit(solution)/shard_map/all_to_all | solution.py:349
  126.0 0.0 copy-done.3
  126.0 2.0 %outer.1 = (bf16[1,256,768]{2,1,0:T(8,128)(2,1)}, bf16[1,256,768]{2,1,0:T(8,128)(2,1)}, bf16[1,256,768]{2,1,0:T(8,128)(2,1)}, f32[64,256]{1,0:T(8,128)S(1)}) custom-call(s32[2,256]{1,0:T(2,128)S(1)} %bitcast.8, bf16[8,440,128]{2,1,0:T(8,128)(2,1)S(1)} %get-tuple-element.50.rows, bf16[64,112,128]{2,1,0:T(8,128)(2,1)S(1)} %all-to-all-done.3.recv), custom_call_target="tpu_custom_call" | custom-call | flops 679477248 | bytes 3538944 | tf_op jit(solution)/shard_map/outer/pallas_call | solution.py:283
  127.9 7.3 %all-to-all-done.4 = f32[64,1,128]{2,1,0:T(1,128)S(1)} async-done(((f32[64,1,128]{2,1,0:T(1,128)}), f32[64,1,128]{2,1,0:T(1,128)S(1)}, u32[]{:S(2)}, u32[]{:S(2)}) %all-to-all-start.4) | async-done | bytes 32800 | tf_op jit(solution)/shard_map/all_to_all | solution.py:349
  135.3 0.8 place.1
Async XLA Ops:
  3.7 15.0 %copy-start = (bf16[1,256,768]{2,1,0:T(8,128)(2,1)S(1)}, bf16[1,256,768]{2,1,0:T(8,128)(2,1)}, u32[]{:S(2)}) copy-start(bf16[1,256,768]{2,1,0:T(8,128)(2,1)} %gate.1) | copy-start | bytes 1179652
  3.7 60.4 %all-to-all-start.3 = ((bf16[64,112,128]{2,1,0:T(8,128)(2,1)}), bf16[64,112,128]{2,1,0:T(8,128)(2,1)S(1)}, u32[]{:S(2)}, u32[]{:S(2)}) async-start(bf16[64,112,128]{2,1,0:T(8,128)(2,1)} %pack.1), calls=%async_computation.3 | async-start | bytes 3670016 | tf_op jit(solution)/shard_map/all_to_all | solution.py:326
  18.7 1.0 copy-start.1
  19.7 1.0 copy-start.2
  66.1 59.8 %copy-start.3 = (s32[256,2]{0,1:T(2,128)S(1)}, s32[256,2]{0,1:T(2,128)}, u32[]{:S(2)}) copy-start(s32[256,2]{0,1:T(2,128)} %param.12) | copy-start | bytes 6148
  118.8 16.5 %all-to-all-start.4 = ((f32[64,1,128]{2,1,0:T(1,128)}), f32[64,1,128]{2,1,0:T(1,128)S(1)}, u32[]{:S(2)}, u32[]{:S(2)}) async-start(f32[64,1,128]{2,1,0:T(1,128)} %bitcast.3), calls=%async_computation.4 | async-start | bytes 65536 | tf_op jit(solution)/shard_map/all_to_all | solution.py:349

commit v5 on v4

--- a/solution.py
+++ b/solution.py
@@ -58,21 +58,9 @@
     pick = jnp.where(spread == slot.astype(f32), 1.0, 0.0)
     pick = pick.reshape(experts * SUB, toks).astype(bf16)
     ninth = jnp.where(rank == float(SUB), 1.0, 0.0).astype(bf16)
-    pieces = [slice(0, half), slice(half, 2 * half), slice(2 * half, 2 * half + 2 * SUB)]
+    pieces = [slice(at, at + 2 * SUB) for at in range(0, 2 * half + 2 * SUB, 2 * SUB)]
     leaving = copies([(out.at[:, p], out_h.at[:, p]) for p in pieces], outs)
     last[...] = jnp.zeros(last.shape, f32)
-    for i, source in enumerate((tokens, grads)):
-        arriving[2 + i].wait()
-        rows = mm(pick, source[...])
-        for c in range(blocks):
-            tile = rows[:, c * LANES : (c + 1) * LANES].reshape(experts, SUB, LANES)
-            at = i * half + c * SUB
-            out[:, at : at + SUB, :] = tile.astype(bf16)
-        leaving[i].start()
-        rows = mm(ninth, source[...])
-        for c in range(blocks):
-            place = i * blocks + c
-            last[place // SUB, pl.ds(place % SUB, experts, stride=SUB), :] = rows[:, c * LANES : (c + 1) * LANES]
     arriving[1].wait()
     prob = combine[...].astype(f32)
     prob = jnp.where(first, prob[0:1, :], jnp.where(second, prob[1:2, :], 0.0))
@@ -83,10 +71,23 @@
         row = jnp.where(lane == r, value, row)
     place = 2 * blocks
     last[place // SUB, pl.ds(place % SUB, experts, stride=SUB), :] = row
+    for i, source in enumerate((tokens, grads)):
+        arriving[2 + i].wait()
+        rows = mm(pick, source[...])
+        for c in range(blocks):
+            tile = rows[:, c * LANES : (c + 1) * LANES].reshape(experts, SUB, LANES)
+            at = i * half + c * SUB
+            out[:, at : at + SUB, :] = tile.astype(bf16)
+            if c % 2:
+                leaving[(i * blocks + c) // 2].start()
+        rows = mm(ninth, source[...])
+        for c in range(blocks):
+            place = i * blocks + c
+            last[place // SUB, pl.ds(place % SUB, experts, stride=SUB), :] = rows[:, c * LANES : (c + 1) * LANES]
     for k in range(2):
         at = 2 * half + k * SUB
         out[:, at : at + SUB, :] = last[k].reshape(experts, SUB, LANES).astype(bf16)
-    leaving[2].start()
+    leaving[-1].start()
     for c in leaving:
         c.wait()
 
@@ -105,7 +106,7 @@
             pltpu.VMEM(shape, bf16),
             pltpu.VMEM((2, experts * SUB, LANES), f32),
             pltpu.SemaphoreType.DMA((4,)),
-            pltpu.SemaphoreType.DMA((3,)),
+            pltpu.SemaphoreType.DMA((width // LANES + 1,)),
         ],
         compiler_params=params(WHOLE),
         name="pack",
@@ -136,10 +137,10 @@
     main = experts * SUB
 
     def tile(at):
-        return recv[:, at : at + SUB, :].astype(f32).reshape(main, LANES)
+        return recv[:, at : at + SUB, :].reshape(main, LANES)
 
     for k in range(2):
-        last[k] = tile((2 * blocks + k) * SUB)
+        last[k] = tile((2 * blocks + k) * SUB).astype(f32)
 
     def taken(place):
         return last[place // SUB, pl.ds(place % SUB, experts, stride=SUB), :]
@@ -147,7 +148,7 @@
     for i, rows in enumerate((rows_x, rows_dy)):
         for c in range(blocks):
             lanes = slice(c * LANES, (c + 1) * LANES)
-            rows[0:main, lanes] = tile((i * blocks + c) * SUB).astype(bf16)
+            rows[0:main, lanes] = tile((i * blocks + c) * SUB)
             rows[main:, lanes] = taken(i * blocks + c).astype(bf16)
     return taken(2 * blocks)
 
@@ -274,7 +275,9 @@
     for i, (other, out) in enumerate(((rows_x, gate), (rows_x, up), (rows_dy, down))):
         value = jnp.concatenate([block(i * per + c) for c in range(per)], axis=1)
         out[0] = mm(value, other[...], ((0,), (0,))).astype(bf16)
-    ranks[...] = rank_of(routes, *ranks.shape)[2]
+    first, second, rank = rank_of(routes, recv.shape[0], routes.shape[1])
+    for k, mine in enumerate((first, second)):
+        ranks[k : k + 1, :] = jnp.sum(jnp.where(mine, rank, 0.0), axis=0, keepdims=True)
 
 
 def outer(routes, rows, recv, hidden, width):
@@ -283,7 +286,7 @@
     return pl.pallas_call(
         outer_kernel,
         out_shape=(jax.ShapeDtypeStruct((1, hidden, width), bf16),) * 3
-        + (jax.ShapeDtypeStruct((experts, routes.shape[1]), f32),),
+        + (jax.ShapeDtypeStruct(routes.shape, f32),),
         scratch_shapes=unpacked(experts, width),
         compiler_params=params(),
         cost_estimate=pl.CostEstimate(
@@ -294,17 +297,15 @@
 
 
 def place_kernel(routes, ranks, scores, out):
-    experts, toks = ranks.shape
-    rank = ranks[...]
-    table = scores[:, 0:TERM] + scores[:, TERM : 2 * TERM] + scores[:, 2 * TERM : 3 * TERM]
-    value = jnp.zeros((experts, toks), f32)
-    for r in range(CAP):
-        value = jnp.where(rank == float(r), table[:, r : r + 1], value)
+    experts, toks = scores.shape[0], routes.shape[1]
+    table = scores[:, 0 : 3 * TERM].astype(bf16)
     e = iota((experts, toks), 0)
+    slot = (iota((3 * TERM, toks), 0) & (TERM - 1)).astype(f32)
     for k in range(2):
-        out[k : k + 1, :] = jnp.sum(
-            jnp.where(e == routes[k : k + 1, :], value, 0.0), axis=0, keepdims=True
-        )
+        hot = jnp.where(e == routes[k : k + 1, :], 1.0, 0.0).astype(bf16)
+        taken = mm(table, hot, ((0,), (0,)))
+        taken = jnp.where(slot == ranks[k : k + 1, :], taken, 0.0)
+        out[k : k + 1, :] = jnp.sum(taken, axis=0, keepdims=True)
 
 
 def place(routes, ranks, scores):

time: 137 us -> 136 us (level)
  no operation moved by 1% of the time
where the time goes in v5:
time: 136 us
  blocking collectives  51.7 us (38%)
  waiting for transfers between devices  50.4 us (37%)
  starting transfers between devices  22.1 us (16%)
  Pallas kernels  8.25 us (6%)
  local copies, waits for them, and re-layouts  2 us (1%)
    all_to_all x1, waiting for transfers between devices, local(): lax.all_to_all(packed, 'expert', split_axis=0, concat_axis=0, tiled=True)  43 us
    all_to_all x1, blocking collectives, exchange(): lax.all_to_all(pieces, both, split_axis=0, concat_axis=0, tiled=True, axi...  27.1 us
    all_gather x1, blocking collectives, odd(): lax.all_gather(mine, both, axis=0, tiled=True, axis_index_groups=lines)  24.6 us
    all_to_all x1, starting transfers between devices, local(): lax.all_to_all(packed, 'expert', split_axis=0, concat_axis=0, tiled=True)  15 us
    all_to_all x1, waiting for transfers between devices, local(): lax.all_to_all(scores, 'expert', split_axis=0, concat_axis=0, tiled=True)  7.34 us
    all_to_all x1, starting transfers between devices, local(): lax.all_to_all(scores, 'expert', split_axis=0, concat_axis=0, tiled=True)  7.16 us
    pallas_call x1, Pallas kernels, pack(): pl.pallas_call(pack_kernel, in_specs=[pl.BlockSpec(memory_space=pltpu.HBM...  3.03 us
  transfers between devices with their start and end apart: 2, of which 2 were waited for; matrix products, arithmetic and copies ran while one was open for 0% of the time, Pallas kernels for 2%

profile of v5, /device:TPU:1, one launch (start us, length us, event | category | flops | bytes accessed | tf_op | source)
XLA Modules:
  0.0 135.8 jit_solution(8440756911752237975)
XLA Ops:
  0.6 3.0 %pack.1 = bf16[64,112,128]{2,1,0:T(8,128)(2,1)} custom-call(s32[2,256]{1,0:T(2,128)} %bitcast.7, bf16[2,256]{1,0:T(2,128)(2,1)} %bitcast.11, bf16[256,768]{1,0:T(8,128)(2,1)} %tokens_h.1, bf16[256,768]{1,0:T(8,128)(2,1)} %grads_h.1), custom_call_target="tpu_custom_call" | custom-call | tf_op jit(solution)/shard_map/pack/pallas_call | solution.py:99
  3.7 0.0 copy-start
  3.7 15.0 %all-to-all-start.3 = ((bf16[64,112,128]{2,1,0:T(8,128)(2,1)}), bf16[64,112,128]{2,1,0:T(8,128)(2,1)S(1)}, u32[]{:S(2)}, u32[]{:S(2)}) async-start(bf16[64,112,128]{2,1,0:T(8,128)(2,1)} %pack.1), calls=%async_computation.3 | async-start | bytes 3670016 | tf_op jit(solution)/shard_map/all_to_all | solution.py:327
  18.7 0.0 copy-done
  18.7 0.0 copy-start.1
  18.7 1.0 copy-done.1
  19.7 0.0 copy-start.2
  19.7 1.0 copy-done.2
  20.7 0.4 stage.1.weights
  21.1 43.0 %all-to-all-done.3.recv = bf16[64,112,128]{2,1,0:T(8,128)(2,1)S(1)} async-done(((bf16[64,112,128]{2,1,0:T(8,128)(2,1)}), bf16[64,112,128]{2,1,0:T(8,128)(2,1)S(1)}, u32[]{:S(2)}, u32[]{:S(2)}) %all-to-all-start.3) | async-done | bytes 1835040 | tf_op jit(solution)/shard_map/all_to_all | solution.py:327
  64.1 1.8 %project.1 = (bf16[8,72,768]{2,1,0:T(8,128)(2,1)S(1)}, f32[72,768]{1,0:T(8,128)S(1)}, f32[64,128]{1,0:T(8,128)S(1)}) custom-call(s32[1]{0:T(128)} %bitcast.1.me, bf16[64,112,128]{2,1,0:T(8,128)(2,1)S(1)} %all-to-all-done.3.recv, bf16[3,768,256]{2,1,0:T(8,128)(2,1)S(1)} %stage.1.weights), custom_call_target="tpu_custom_call" | custom-call | tf_op jit(solution)/shard_map/project/pallas_call | solution.py:187
  65.9 0.0 copy-start.3
  66.0 52.0 %conditional.2 = (bf16[8,440,128]{2,1,0:T(8,128)(2,1)S(1)}) conditional(s32[]{:T(128)} %convert_element_type.6, (bf16[8,72,768]{2,1,0:T(8,128)(2,1)S(1)}, s32[1]{0:T(128)}, f32[72,768]{1,0:T(8,128)S(1)}, f32[64,128]{1,0:T(8,128)S(1)}) %tuple.23, (bf16[8,72,768]{2,1,0:T(8,128)(2,1)S(1)}, s32[1]{0:T(128)}, f32[72,768]{1,0:T(8,128)S(1)}, ...), branch_computations={%region_0.1_spmd, %region_1.2_spmd} | conditional | bytes 3571720
  66.0 27.1 %all_to_all.22.parts = bf16[8,72,768]{2,1,0:T(8,128)(2,1)S(1)} all-to-all(bf16[8,72,768]{2,1,0:T(8,128)(2,1)S(1)} %get-tuple-element.25), channel_id=1, replica_groups={{0,1,2,3,4,5,6,7},{13,12,11,10,9,8,15,14},{16,17,18,19,20,21,22,23},{29..., dimensions={0} | all-to-all | bytes 1769472 | tf_op jit(solution)/shard_map/cond/branch_0_fun/all_to_all | solution.py:335
  93.0 0.3 terms.2
  93.3 24.6 %all_gather.2 = bf16[8,440,128]{2,1,0:T(8,128)(2,1)S(1)} all-gather(bf16[1,440,128]{2,1,0:T(8,128)(2,1)S(1)} %terms.2), channel_id=1, replica_groups={{0,1,2,3,4,5,6,7},{13,12,11,10,9,8,15,14},{16,17,18,19,20,21,22,23},{29..., dimensions={0}, use_global_device_ids=true | all-gather | bytes 1013760 | tf_op jit(solution)/shard_map/cond/branch_0_fun/all_gather | solution.py:347
  118.0 0.6 slice_convert_fusion
  118.6 7.2 %all-to-all-start.4 = ((f32[64,1,128]{2,1,0:T(1,128)}), f32[64,1,128]{2,1,0:T(1,128)S(1)}, u32[]{:S(2)}, u32[]{:S(2)}) async-start(f32[64,1,128]{2,1,0:T(1,128)} %bitcast.3), calls=%async_computation.4 | async-start | bytes 65536 | tf_op jit(solution)/shard_map/all_to_all | solution.py:350
  125.8 0.0 copy-done.3
  125.8 1.9 %outer.1 = (bf16[1,256,768]{2,1,0:T(8,128)(2,1)}, bf16[1,256,768]{2,1,0:T(8,128)(2,1)}, bf16[1,256,768]{2,1,0:T(8,128)(2,1)}, f32[2,256]{1,0:T(2,128)S(1)}) custom-call(s32[2,256]{1,0:T(2,128)S(1)} %bitcast.8, bf16[8,440,128]{2,1,0:T(8,128)(2,1)S(1)} %get-tuple-element.50.rows, bf16[64,112,128]{2,1,0:T(8,128)(2,1)S(1)} %all-to-all-done.3.recv), custom_call_target="tpu_custom_call" | custom-call | flops 679477248 | bytes 3538944 | tf_op jit(solution)/shard_map/outer/pallas_call | solution.py:286
  127.7 7.3 %all-to-all-done.4 = f32[64,1,128]{2,1,0:T(1,128)S(1)} async-done(((f32[64,1,128]{2,1,0:T(1,128)}), f32[64,1,128]{2,1,0:T(1,128)S(1)}, u32[]{:S(2)}, u32[]{:S(2)}) %all-to-all-start.4) | async-done | bytes 32800 | tf_op jit(solution)/shard_map/all_to_all | solution.py:350
  135.0 0.8 place.1
Async XLA Ops:
  3.7 15.0 %copy-start = (bf16[1,256,768]{2,1,0:T(8,128)(2,1)S(1)}, bf16[1,256,768]{2,1,0:T(8,128)(2,1)}, u32[]{:S(2)}) copy-start(bf16[1,256,768]{2,1,0:T(8,128)(2,1)} %gate.1) | copy-start | bytes 1179652
  3.7 60.4 %all-to-all-start.3 = ((bf16[64,112,128]{2,1,0:T(8,128)(2,1)}), bf16[64,112,128]{2,1,0:T(8,128)(2,1)S(1)}, u32[]{:S(2)}, u32[]{:S(2)}) async-start(bf16[64,112,128]{2,1,0:T(8,128)(2,1)} %pack.1), calls=%async_computation.3 | async-start | bytes 3670016 | tf_op jit(solution)/shard_map/all_to_all | solution.py:327
  18.7 1.0 copy-start.1
  19.7 1.0 copy-start.2
  65.9 59.8 %copy-start.3 = (s32[256,2]{0,1:T(2,128)S(1)}, s32[256,2]{0,1:T(2,128)}, u32[]{:S(2)}) copy-start(s32[256,2]{0,1:T(2,128)} %param.12) | copy-start | bytes 6148
  118.6 16.5 %all-to-all-start.4 = ((f32[64,1,128]{2,1,0:T(1,128)}), f32[64,1,128]{2,1,0:T(1,128)S(1)}, u32[]{:S(2)}, u32[]{:S(2)}) async-start(f32[64,1,128]{2,1,0:T(1,128)} %bitcast.3), calls=%async_computation.4 | async-start | bytes 65536 | tf_op jit(solution)/shard_map/all_to_all | solution.py:350

commit v6 on v5

--- a/solution.py
+++ b/solution.py
@@ -321,15 +321,18 @@
     experts, groups = lax.axis_size("expert"), lax.axis_size("dp")
     hidden = w_gate.shape[1]
     y, core = lax.axis_index("dp").astype(i32), lax.axis_index("expert").astype(i32) & 1
-    me = jnp.where(core == 1, lax.rem(TURN + groups - y, groups), y).reshape(1)
+    ends = jnp.where(2 * y < groups, 2 * y, 2 * (groups - y) - 1)
+    me = jnp.where(core == 1, lax.rem(TURN + groups - y, groups), ends).reshape(1)
     by_slot = routes.T
     packed = pack(by_slot, combine.T, tokens, grad_out, experts)
     recv = lax.all_to_all(packed, "expert", split_axis=0, concat_axis=0, tiled=True)
     part, own, probs = project(me, recv, stage(w_gate, w_up, w_down), groups)
+    orders = (
+        [groups - 1 - j // 2 if j % 2 else j // 2 for j in range(groups)],
+        [(TURN - j) % groups for j in range(groups)],
+    )
     both = ("expert", "dp")
-    lines = [
-        [e * groups + ((TURN - j) % groups if e % 2 else j) for j in range(groups)] for e in range(experts)
-    ]
+    lines = [[e * groups + place for place in orders[e % 2]] for e in range(experts)]
 
     def exchange(pieces):
         return lax.all_to_all(

time: 136 us -> 136 us (level)
  starting transfers between devices: 22.1 us -> 20.7 us
    all_to_all x1, starting transfers between devices: 7.16 us -> 5.72 us  [local(): lax.all_to_all(scores, 'expert', split_axis=0, concat_axis=0, tiled=True)]
where the time goes in v6:
time: 136 us; the launch traced here: 135 us
  blocking collectives  52.7 us (39%)
  waiting for transfers between devices  50.4 us (37%)
  starting transfers between devices  20.7 us (15%)
  Pallas kernels  8.25 us (6%)
  local copies, waits for them, and re-layouts  2 us (1%)
    all_to_all x1, waiting for transfers between devices, local(): lax.all_to_all(packed, 'expert', split_axis=0, concat_axis=0, tiled=True)  43 us
    all_to_all x1, blocking collectives, exchange(): lax.all_to_all(pieces, both, split_axis=0, concat_axis=0, tiled=True, axi...  27.4 us
    all_gather x1, blocking collectives, odd(): lax.all_gather(mine, both, axis=0, tiled=True, axis_index_groups=lines)  25.3 us
    all_to_all x1, starting transfers between devices, local(): lax.all_to_all(packed, 'expert', split_axis=0, concat_axis=0, tiled=True)  15 us
    all_to_all x1, waiting for transfers between devices, local(): lax.all_to_all(scores, 'expert', split_axis=0, concat_axis=0, tiled=True)  7.34 us
    all_to_all x1, starting transfers between devices, local(): lax.all_to_all(scores, 'expert', split_axis=0, concat_axis=0, tiled=True)  5.72 us
    pallas_call x1, Pallas kernels, pack(): pl.pallas_call(pack_kernel, in_specs=[pl.BlockSpec(memory_space=pltpu.HBM...  3.03 us
  transfers between devices with their start and end apart: 2, of which 2 were waited for; matrix products, arithmetic and copies ran while one was open for 0% of the time, Pallas kernels for 2%

profile of v6, /device:TPU:1, one launch (start us, length us, event | category | flops | bytes accessed | tf_op | source)
XLA Modules:
  0.0 135.4 jit_solution(5119223361337014793)
XLA Ops:
  0.6 3.0 %pack.1 = bf16[64,112,128]{2,1,0:T(8,128)(2,1)} custom-call(s32[2,256]{1,0:T(2,128)} %bitcast.7, bf16[2,256]{1,0:T(2,128)(2,1)} %bitcast.11, bf16[256,768]{1,0:T(8,128)(2,1)} %tokens_h.1, bf16[256,768]{1,0:T(8,128)(2,1)} %grads_h.1), custom_call_target="tpu_custom_call" | custom-call | tf_op jit(solution)/shard_map/pack/pallas_call | solution.py:99
  3.7 0.0 copy-start
  3.7 15.0 %all-to-all-start.3 = ((bf16[64,112,128]{2,1,0:T(8,128)(2,1)}), bf16[64,112,128]{2,1,0:T(8,128)(2,1)S(1)}, u32[]{:S(2)}, u32[]{:S(2)}) async-start(bf16[64,112,128]{2,1,0:T(8,128)(2,1)} %pack.1), calls=%async_computation.3 | async-start | bytes 3670016 | tf_op jit(solution)/shard_map/all_to_all | solution.py:328
  18.7 0.0 copy-done
  18.7 0.0 copy-start.1
  18.7 1.0 copy-done.1
  19.7 0.0 copy-start.2
  19.7 1.0 copy-done.2
  20.7 0.4 stage.1.weights
  21.1 43.0 %all-to-all-done.3.recv = bf16[64,112,128]{2,1,0:T(8,128)(2,1)S(1)} async-done(((bf16[64,112,128]{2,1,0:T(8,128)(2,1)}), bf16[64,112,128]{2,1,0:T(8,128)(2,1)S(1)}, u32[]{:S(2)}, u32[]{:S(2)}) %all-to-all-start.3) | async-done | bytes 1835040 | tf_op jit(solution)/shard_map/all_to_all | solution.py:328
  64.1 1.8 %project.1 = (bf16[8,72,768]{2,1,0:T(8,128)(2,1)S(1)}, f32[72,768]{1,0:T(8,128)S(1)}, f32[64,128]{1,0:T(8,128)S(1)}) custom-call(s32[1]{0:T(128)} %bitcast.1.me, bf16[64,112,128]{2,1,0:T(8,128)(2,1)S(1)} %all-to-all-done.3.recv, bf16[3,768,256]{2,1,0:T(8,128)(2,1)S(1)} %stage.1.weights), custom_call_target="tpu_custom_call" | custom-call | tf_op jit(solution)/shard_map/project/pallas_call | solution.py:187
  65.9 0.0 copy-start.3
  66.0 53.0 %conditional.2 = (bf16[8,440,128]{2,1,0:T(8,128)(2,1)S(1)}) conditional(s32[]{:T(128)} %convert_element_type.6, (bf16[8,72,768]{2,1,0:T(8,128)(2,1)S(1)}, s32[1]{0:T(128)}, f32[72,768]{1,0:T(8,128)S(1)}, f32[64,128]{1,0:T(8,128)S(1)}) %tuple.23, (bf16[8,72,768]{2,1,0:T(8,128)(2,1)S(1)}, s32[1]{0:T(128)}, f32[72,768]{1,0:T(8,128)S(1)}, ...), branch_computations={%region_0.1_spmd, %region_1.2_spmd} | conditional | bytes 3571720
  66.0 27.4 %all_to_all.22.parts = bf16[8,72,768]{2,1,0:T(8,128)(2,1)S(1)} all-to-all(bf16[8,72,768]{2,1,0:T(8,128)(2,1)S(1)} %get-tuple-element.25), channel_id=1, replica_groups={{0,7,1,6,2,5,3,4},{13,12,11,10,9,8,15,14},{16,23,17,22,18,21,19,20},{29..., dimensions={0} | all-to-all | bytes 1769472 | tf_op jit(solution)/shard_map/cond/branch_0_fun/all_to_all | solution.py:338
  93.4 0.3 terms.2
  93.7 25.3 %all_gather.2 = bf16[8,440,128]{2,1,0:T(8,128)(2,1)S(1)} all-gather(bf16[1,440,128]{2,1,0:T(8,128)(2,1)S(1)} %terms.2), channel_id=1, replica_groups={{0,7,1,6,2,5,3,4},{13,12,11,10,9,8,15,14},{16,23,17,22,18,21,19,20},{29..., dimensions={0}, use_global_device_ids=true | all-gather | bytes 1013760 | tf_op jit(solution)/shard_map/cond/branch_0_fun/all_gather | solution.py:350
  119.0 0.6 slice_convert_fusion
  119.6 5.7 %all-to-all-start.4 = ((f32[64,1,128]{2,1,0:T(1,128)}), f32[64,1,128]{2,1,0:T(1,128)S(1)}, u32[]{:S(2)}, u32[]{:S(2)}) async-start(f32[64,1,128]{2,1,0:T(1,128)} %bitcast.3), calls=%async_computation.4 | async-start | bytes 65536 | tf_op jit(solution)/shard_map/all_to_all | solution.py:353
  125.3 0.0 copy-done.3
  125.3 1.9 %outer.1 = (bf16[1,256,768]{2,1,0:T(8,128)(2,1)}, bf16[1,256,768]{2,1,0:T(8,128)(2,1)}, bf16[1,256,768]{2,1,0:T(8,128)(2,1)}, f32[2,256]{1,0:T(2,128)S(1)}) custom-call(s32[2,256]{1,0:T(2,128)S(1)} %bitcast.8, bf16[8,440,128]{2,1,0:T(8,128)(2,1)S(1)} %get-tuple-element.50.rows, bf16[64,112,128]{2,1,0:T(8,128)(2,1)S(1)} %all-to-all-done.3.recv), custom_call_target="tpu_custom_call" | custom-call | flops 679477248 | bytes 3538944 | tf_op jit(solution)/shard_map/outer/pallas_call | solution.py:286
  127.2 7.3 %all-to-all-done.4 = f32[64,1,128]{2,1,0:T(1,128)S(1)} async-done(((f32[64,1,128]{2,1,0:T(1,128)}), f32[64,1,128]{2,1,0:T(1,128)S(1)}, u32[]{:S(2)}, u32[]{:S(2)}) %all-to-all-start.4) | async-done | bytes 32800 | tf_op jit(solution)/shard_map/all_to_all | solution.py:353
  134.6 0.8 place.1
Async XLA Ops:
  3.7 15.0 %copy-start = (bf16[1,256,768]{2,1,0:T(8,128)(2,1)S(1)}, bf16[1,256,768]{2,1,0:T(8,128)(2,1)}, u32[]{:S(2)}) copy-start(bf16[1,256,768]{2,1,0:T(8,128)(2,1)} %gate.1) | copy-start | bytes 1179652
  3.7 60.4 %all-to-all-start.3 = ((bf16[64,112,128]{2,1,0:T(8,128)(2,1)}), bf16[64,112,128]{2,1,0:T(8,128)(2,1)S(1)}, u32[]{:S(2)}, u32[]{:S(2)}) async-start(bf16[64,112,128]{2,1,0:T(8,128)(2,1)} %pack.1), calls=%async_computation.3 | async-start | bytes 3670016 | tf_op jit(solution)/shard_map/all_to_all | solution.py:328
  18.7 1.0 copy-start.1
  19.7 1.0 copy-start.2
  65.9 59.4 %copy-start.3 = (s32[256,2]{0,1:T(2,128)S(1)}, s32[256,2]{0,1:T(2,128)}, u32[]{:S(2)}) copy-start(s32[256,2]{0,1:T(2,128)} %param.12) | copy-start | bytes 6148
  119.6 15.0 %all-to-all-start.4 = ((f32[64,1,128]{2,1,0:T(1,128)}), f32[64,1,128]{2,1,0:T(1,128)S(1)}, u32[]{:S(2)}, u32[]{:S(2)}) async-start(f32[64,1,128]{2,1,0:T(1,128)} %bitcast.3), calls=%async_computation.4 | async-start | bytes 65536 | tf_op jit(solution)/shard_map/all_to_all | solution.py:353

commit v7 on v5

--- a/solution.py
+++ b/solution.py
@@ -115,14 +115,15 @@
 
 def stage_kernel(gate, up, down, out):
     for i, weight in enumerate((gate, up, down)):
-        out[i] = weight[0].astype(f32).T.astype(bf16)
+        hidden = weight.shape[1]
+        out[:, i * hidden : (i + 1) * hidden] = weight[0].astype(f32).T.astype(bf16)
 
 
 def stage(*weights):
     _, hidden, width = weights[0].shape
     return pl.pallas_call(
         stage_kernel,
-        out_shape=jax.ShapeDtypeStruct((len(weights), width, hidden), bf16),
+        out_shape=jax.ShapeDtypeStruct((width, len(weights) * hidden), bf16),
         compiler_params=params(),
         cost_estimate=pl.CostEstimate(
             flops=3 * width * hidden, bytes_accessed=12 * width * hidden, transcendentals=0
@@ -155,13 +156,12 @@
 
 def project_kernel(me, recv, weights, part, own, probs, rows_x, rows_dy, last):
     groups = part.shape[0]
-    _, width, hidden = weights.shape
+    hidden = weights.shape[1] // 3
     main = recv.shape[0] * SUB
     share = main // groups
     probs[...] = unpack(recv, rows_x, rows_dy, last)
-    for i, rows in enumerate((rows_x, rows_x, rows_dy)):
-        lanes = slice(i * hidden, (i + 1) * hidden)
-        value = mm(rows[...], weights[i])
+    for rows, lanes in ((rows_x, slice(0, 2 * hidden)), (rows_dy, slice(2 * hidden, 3 * hidden))):
+        value = mm(rows[...], weights[:, lanes])
         for j in range(groups):
             piece = jnp.concatenate(
                 [value[j * share : (j + 1) * share], value[main + j * SUB : main + (j + 1) * SUB]]
@@ -180,7 +180,7 @@
 
 def project(me, recv, weights, groups):
     experts = recv.shape[0]
-    _, width, hidden = weights.shape
+    width, hidden = weights.shape[0], weights.shape[1] // 3
     total = experts * CAP
     count = total // groups
     vmem = pl.BlockSpec(memory_space=pltpu.VMEM)

time: 136 us -> 136 us (level)
  no operation moved by 1% of the time
where the time goes in v7:
time: 136 us
  blocking collectives  51.7 us (38%)
  waiting for transfers between devices  50.4 us (37%)
  starting transfers between devices  22.2 us (16%)
  Pallas kernels  8.07 us (6%)
  local copies, waits for them, and re-layouts  2 us (1%)
    all_to_all x1, waiting for transfers between devices, local(): lax.all_to_all(packed, 'expert', split_axis=0, concat_axis=0, tiled=True)  43 us
    all_to_all x1, blocking collectives, exchange(): lax.all_to_all(pieces, both, split_axis=0, concat_axis=0, tiled=True, axi...  27.1 us
    all_gather x1, blocking collectives, odd(): lax.all_gather(mine, both, axis=0, tiled=True, axis_index_groups=lines)  24.6 us
    all_to_all x1, starting transfers between devices, local(): lax.all_to_all(packed, 'expert', split_axis=0, concat_axis=0, tiled=True)  15 us
    all_to_all x1, waiting for transfers between devices, local(): lax.all_to_all(scores, 'expert', split_axis=0, concat_axis=0, tiled=True)  7.34 us
    all_to_all x1, starting transfers between devices, local(): lax.all_to_all(scores, 'expert', split_axis=0, concat_axis=0, tiled=True)  7.22 us
    pallas_call x1, Pallas kernels, pack(): pl.pallas_call(pack_kernel, in_specs=[pl.BlockSpec(memory_space=pltpu.HBM...  3.03 us
  transfers between devices with their start and end apart: 2, of which 2 were waited for; matrix products, arithmetic and copies ran while one was open for 0% of the time, Pallas kernels for 2%

profile of v7, /device:TPU:1, one launch (start us, length us, event | category | flops | bytes accessed | tf_op | source)
XLA Modules:
  0.0 135.7 jit_solution(869384175928830936)
XLA Ops:
  0.6 3.0 %pack.1 = bf16[64,112,128]{2,1,0:T(8,128)(2,1)} custom-call(s32[2,256]{1,0:T(2,128)} %bitcast.7, bf16[2,256]{1,0:T(2,128)(2,1)} %bitcast.11, bf16[256,768]{1,0:T(8,128)(2,1)} %tokens_h.1, bf16[256,768]{1,0:T(8,128)(2,1)} %grads_h.1), custom_call_target="tpu_custom_call" | custom-call | tf_op jit(solution)/shard_map/pack/pallas_call | solution.py:99
  3.7 0.0 copy-start
  3.7 15.0 %all-to-all-start.3 = ((bf16[64,112,128]{2,1,0:T(8,128)(2,1)}), bf16[64,112,128]{2,1,0:T(8,128)(2,1)S(1)}, u32[]{:S(2)}, u32[]{:S(2)}) async-start(bf16[64,112,128]{2,1,0:T(8,128)(2,1)} %pack.1), calls=%async_computation.3 | async-start | bytes 3670016 | tf_op jit(solution)/shard_map/all_to_all | solution.py:327
  18.7 0.0 copy-done
  18.7 0.0 copy-start.1
  18.7 1.0 copy-done.1
  19.7 0.0 copy-start.2
  19.7 1.0 copy-done.2
  20.7 0.4 stage.1.weights
  21.1 43.0 %all-to-all-done.3.recv = bf16[64,112,128]{2,1,0:T(8,128)(2,1)S(1)} async-done(((bf16[64,112,128]{2,1,0:T(8,128)(2,1)}), bf16[64,112,128]{2,1,0:T(8,128)(2,1)S(1)}, u32[]{:S(2)}, u32[]{:S(2)}) %all-to-all-start.3) | async-done | bytes 1835040 | tf_op jit(solution)/shard_map/all_to_all | solution.py:327
  64.1 1.7 %project.1 = (bf16[8,72,768]{2,1,0:T(8,128)(2,1)S(1)}, f32[72,768]{1,0:T(8,128)S(1)}, f32[64,128]{1,0:T(8,128)S(1)}) custom-call(s32[1]{0:T(128)} %bitcast.1.me, bf16[64,112,128]{2,1,0:T(8,128)(2,1)S(1)} %all-to-all-done.3.recv, bf16[768,768]{1,0:T(8,128)(2,1)S(1)} %stage.1.weights), custom_call_target="tpu_custom_call" | custom-call | tf_op jit(solution)/shard_map/project/pallas_call | solution.py:187
  65.8 0.0 copy-start.3
  65.8 52.0 %conditional.2 = (bf16[8,440,128]{2,1,0:T(8,128)(2,1)S(1)}) conditional(s32[]{:T(128)} %convert_element_type.6, (bf16[8,72,768]{2,1,0:T(8,128)(2,1)S(1)}, s32[1]{0:T(128)}, f32[72,768]{1,0:T(8,128)S(1)}, f32[64,128]{1,0:T(8,128)S(1)}) %tuple.23, (bf16[8,72,768]{2,1,0:T(8,128)(2,1)S(1)}, s32[1]{0:T(128)}, f32[72,768]{1,0:T(8,128)S(1)}, ...), branch_computations={%region_0.1_spmd, %region_1.2_spmd} | conditional | bytes 3571720
  65.8 27.1 %all_to_all.22.parts = bf16[8,72,768]{2,1,0:T(8,128)(2,1)S(1)} all-to-all(bf16[8,72,768]{2,1,0:T(8,128)(2,1)S(1)} %get-tuple-element.25), channel_id=1, replica_groups={{0,1,2,3,4,5,6,7},{13,12,11,10,9,8,15,14},{16,17,18,19,20,21,22,23},{29..., dimensions={0} | all-to-all | bytes 1769472 | tf_op jit(solution)/shard_map/cond/branch_0_fun/all_to_all | solution.py:335
  92.8 0.3 terms.2
  93.2 24.6 %all_gather.2 = bf16[8,440,128]{2,1,0:T(8,128)(2,1)S(1)} all-gather(bf16[1,440,128]{2,1,0:T(8,128)(2,1)S(1)} %terms.2), channel_id=1, replica_groups={{0,1,2,3,4,5,6,7},{13,12,11,10,9,8,15,14},{16,17,18,19,20,21,22,23},{29..., dimensions={0}, use_global_device_ids=true | all-gather | bytes 1013760 | tf_op jit(solution)/shard_map/cond/branch_0_fun/all_gather | solution.py:347
  117.8 0.6 slice_convert_fusion
  118.4 7.2 %all-to-all-start.4 = ((f32[64,1,128]{2,1,0:T(1,128)}), f32[64,1,128]{2,1,0:T(1,128)S(1)}, u32[]{:S(2)}, u32[]{:S(2)}) async-start(f32[64,1,128]{2,1,0:T(1,128)} %bitcast.3), calls=%async_computation.4 | async-start | bytes 65536 | tf_op jit(solution)/shard_map/all_to_all | solution.py:350
  125.6 0.0 copy-done.3
  125.7 1.9 %outer.1 = (bf16[1,256,768]{2,1,0:T(8,128)(2,1)}, bf16[1,256,768]{2,1,0:T(8,128)(2,1)}, bf16[1,256,768]{2,1,0:T(8,128)(2,1)}, f32[2,256]{1,0:T(2,128)S(1)}) custom-call(s32[2,256]{1,0:T(2,128)S(1)} %bitcast.8, bf16[8,440,128]{2,1,0:T(8,128)(2,1)S(1)} %get-tuple-element.50.rows, bf16[64,112,128]{2,1,0:T(8,128)(2,1)S(1)} %all-to-all-done.3.recv), custom_call_target="tpu_custom_call" | custom-call | flops 679477248 | bytes 3538944 | tf_op jit(solution)/shard_map/outer/pallas_call | solution.py:286
  127.6 7.3 %all-to-all-done.4 = f32[64,1,128]{2,1,0:T(1,128)S(1)} async-done(((f32[64,1,128]{2,1,0:T(1,128)}), f32[64,1,128]{2,1,0:T(1,128)S(1)}, u32[]{:S(2)}, u32[]{:S(2)}) %all-to-all-start.4) | async-done | bytes 32800 | tf_op jit(solution)/shard_map/all_to_all | solution.py:350
  134.9 0.8 place.1
Async XLA Ops:
  3.7 15.0 %copy-start = (bf16[1,256,768]{2,1,0:T(8,128)(2,1)S(1)}, bf16[1,256,768]{2,1,0:T(8,128)(2,1)}, u32[]{:S(2)}) copy-start(bf16[1,256,768]{2,1,0:T(8,128)(2,1)} %gate.1) | copy-start | bytes 1179652
  3.7 60.4 %all-to-all-start.3 = ((bf16[64,112,128]{2,1,0:T(8,128)(2,1)}), bf16[64,112,128]{2,1,0:T(8,128)(2,1)S(1)}, u32[]{:S(2)}, u32[]{:S(2)}) async-start(bf16[64,112,128]{2,1,0:T(8,128)(2,1)} %pack.1), calls=%async_computation.3 | async-start | bytes 3670016 | tf_op jit(solution)/shard_map/all_to_all | solution.py:327
  18.7 1.0 copy-start.1
  19.7 1.0 copy-start.2
  65.8 59.9 %copy-start.3 = (s32[256,2]{0,1:T(2,128)S(1)}, s32[256,2]{0,1:T(2,128)}, u32[]{:S(2)}) copy-start(s32[256,2]{0,1:T(2,128)} %param.12) | copy-start | bytes 6148
  118.4 16.5 %all-to-all-start.4 = ((f32[64,1,128]{2,1,0:T(1,128)}), f32[64,1,128]{2,1,0:T(1,128)S(1)}, u32[]{:S(2)}, u32[]{:S(2)}) async-start(f32[64,1,128]{2,1,0:T(1,128)} %bitcast.3), calls=%async_computation.4 | async-start | bytes 65536 | tf_op jit(solution)/shard_map/all_to_all | solution.py:350
